TPU v7x, 256 devices: a whole 4x4x8 slice. The times are simulated.
256 devices in a mesh: grp: 16 (over x_hi, z), blk: 16 (over y, x_lo, core).
Axes of the slice: x: 4 (x_hi: 2, x_lo: 2; x = x_hi * 2 + x_lo), y: 4, z: 8, core: 2. Of those that a mesh axis runs over, the one named last changes fastest.
Arguments:
- queries: bfloat16 [32768, 2048], P(('grp', 'blk')), parts along dimension 0, may hold values from -8 to 8
- keys: bfloat16 [32768, 1024], P(('grp', 'blk')), parts along dimension 0, may hold values from -8 to 8
- values: bfloat16 [32768, 1024], P(('grp', 'blk')), parts along dimension 0, may hold values from -6 to 6
- dout: bfloat16 [32768, 2048], P(('grp', 'blk')), parts along dimension 0, may hold values from -6 to 6
- segments: int32 [32768], P(('grp', 'blk')), parts along dimension 0, may hold values from 0 to 7, never falling along the last dimension, each value on 1 to 1024 neighbouring positions
Outputs:
- grad_queries: bfloat16 [32768, 2048], P(('grp', 'blk')), parts along dimension 0
- keys_gradient: bfloat16 [32768, 1024], P(('grp', 'blk')), parts along dimension 0
- values_gradient: bfloat16 [32768, 1024], P(('grp', 'blk')), parts along dimension 0
There are 16 independent parts, one for each index of `grp`. A program takes and returns all parts, laid end to end along the dimension named above; each array names one. Nothing has to cross between parts.
Inputs may be any that keep to these rules, and one draw needn't show every extreme that they name: segments never fall along the sequence; each of the 8 documents has 1 to 1024 tokens and one has exactly 1024.
All inputs are finite; a program needn't handle non-finite values.
Results may differ from a plain program's by a relative error of at most 0.015.
Values may be sent and summed in bfloat16 or wider, within the bound.
No kernel may reach another device: no remote copies, remote signals or barrier semaphores. Data moves between devices by JAX's collectives and lax.ppermute only.
A program may use at most 128 MiB of HBM per device.

v0:
```python
import jax
import jax.numpy as jnp
from jax import lax
from jax.sharding import PartitionSpec as P

HQ = 16
KV_HEAD_COUNT = 8
HEAD_SIZE = 128
QUERY_PER_KV = 2
DOCS = 8


score_scale = 1.0 / 12.0
cap_value = 50.0


def scores(
    rows_of_queries, output_grad_rows, rows_of_keys, rows_of_values, query_pos, query_first, key_pos
):
    query_count_total = rows_of_queries.shape[0]
    key_count_total = rows_of_keys.shape[0]
    heads_of_queries = rows_of_queries.reshape(
        query_count_total, KV_HEAD_COUNT, QUERY_PER_KV, HEAD_SIZE
    )
    output_grad_heads = output_grad_rows.reshape(
        query_count_total, KV_HEAD_COUNT, QUERY_PER_KV, HEAD_SIZE
    )
    heads_of_keys = rows_of_keys.reshape(key_count_total, KV_HEAD_COUNT, HEAD_SIZE)
    heads_of_values = rows_of_values.reshape(key_count_total, KV_HEAD_COUNT, HEAD_SIZE)
    raw = jnp.einsum(
        "igrd,jgd->grij", heads_of_queries, heads_of_keys, preferred_element_type=jnp.float32
    )
    capped = jnp.tanh(raw * score_scale / cap_value)
    visible = (key_pos[None, :] <= query_pos[:, None]) & (key_pos[None, :] >= query_first[:, None])
    expo = jnp.where(visible, jnp.exp(cap_value * capped), jnp.float32(0.0))
    dprob = jnp.einsum(
        "igrd,jgd->grij", output_grad_heads, heads_of_values, preferred_element_type=jnp.float32
    )
    return (heads_of_queries, output_grad_heads, heads_of_keys, capped, expo, dprob)


def grads_of(capped, expo, dprob, totals, deltas):
    prob = expo / totals[..., None]
    prob_low = prob.astype(jnp.bfloat16)
    dscore = prob * (dprob - deltas[..., None]) * (1.0 - capped * capped) * score_scale
    return (prob_low, dscore.astype(jnp.bfloat16))


def body(queries, keys, values, dout, segments):
    local_rows = queries.shape[0]
    token_length = local_rows * lax.axis_size("blk")
    offset = lax.axis_index("blk") * local_rows
    labels = jnp.arange(DOCS, dtype=jnp.int32)
    below = (segments[:, None] < labels[None, :]).astype(jnp.float32)
    starts = lax.psum(jnp.sum(below, axis=0), "blk").astype(jnp.int32)
    query_pos = offset + jnp.arange(local_rows, dtype=jnp.int32)
    query_first = jnp.sum(
        jnp.where(segments[:, None] == labels[None, :], starts[None, :], 0), axis=1
    )
    full_keys, full_values = (
        lax.all_gather(keys, "blk", axis=0, tiled=True),
        lax.all_gather(values, "blk", axis=0, tiled=True),
    )
    block_row_span = min(512, token_length)
    block_count = token_length // block_row_span
    key_blocks = full_keys.reshape(block_count, block_row_span, keys.shape[1])
    value_blocks = full_values.reshape(block_count, block_row_span, values.shape[1])
    block_bases = jnp.arange(block_count, dtype=jnp.int32) * block_row_span
    empty_row_stats = jnp.zeros((KV_HEAD_COUNT, QUERY_PER_KV, local_rows), jnp.float32)

    def stats_step(state_now, block_in):
        key_block, value_block, block_base = block_in
        key_pos = block_base + jnp.arange(block_row_span, dtype=jnp.int32)
        parts = scores(queries, dout, key_block, value_block, query_pos, query_first, key_pos)
        expo = parts[4]
        dprob = parts[5]
        return (
            (state_now[0] + jnp.sum(expo, axis=-1), state_now[1] + jnp.sum(expo * dprob, axis=-1)),
            None,
        )

    stats_pair, unused_stats = lax.scan(
        stats_step, (empty_row_stats, empty_row_stats), (key_blocks, value_blocks, block_bases)
    )
    totals = stats_pair[0]
    deltas = stats_pair[1] / totals

    def make_step():

        def grads_step(accum_now, block_in):
            key_block, value_block, block_base = block_in
            key_pos = block_base + jnp.arange(block_row_span, dtype=jnp.int32)
            heads_of_queries, output_grad_heads, heads_of_keys, capped, expo, dprob = scores(
                queries, dout, key_block, value_block, query_pos, query_first, key_pos
            )
            prob_low, dscore_low = grads_of(capped, expo, dprob, totals, deltas)
            new_accum = accum_now + jnp.einsum(
                "grij,jgd->igrd", dscore_low, heads_of_keys, preferred_element_type=jnp.float32
            )
            key_term = jnp.einsum(
                "grij,igrd->jgd", dscore_low, heads_of_queries, preferred_element_type=jnp.float32
            )
            value_term = jnp.einsum(
                "grij,igrd->jgd", prob_low, output_grad_heads, preferred_element_type=jnp.float32
            )
            joined = jnp.concatenate((key_term, value_term), axis=1).reshape(
                block_row_span, 2 * KV_HEAD_COUNT * HEAD_SIZE
            )
            return (new_accum, joined)

        return grads_step

    empty_query_grad = jnp.zeros((local_rows, KV_HEAD_COUNT, QUERY_PER_KV, HEAD_SIZE), jnp.float32)
    grad_query, key_partial_terms = lax.scan(
        make_step(), empty_query_grad, (key_blocks, value_blocks, block_bases)
    )
    reduced_sum = lax.psum_scatter(
        key_partial_terms.reshape(token_length, 2 * KV_HEAD_COUNT * HEAD_SIZE).astype(jnp.bfloat16),
        "blk",
        scatter_dimension=0,
        tiled=True,
    ).astype(jnp.float32)
    keys_gradient = reduced_sum[:, : KV_HEAD_COUNT * HEAD_SIZE].astype(jnp.bfloat16)
    values_gradient = reduced_sum[:, KV_HEAD_COUNT * HEAD_SIZE :].astype(jnp.bfloat16)
    grad_queries = grad_query.reshape(local_rows, HQ * HEAD_SIZE).astype(jnp.bfloat16)
    return (grad_queries, keys_gradient, values_gradient)


def solution(mesh):
    in_specs = (
        P(("grp", "blk"), None),
        P(("grp", "blk"), None),
        P(("grp", "blk"), None),
        P(("grp", "blk"), None),
        P(("grp", "blk")),
    )
    out_specs = (P(("grp", "blk"), None), P(("grp", "blk"), None), P(("grp", "blk"), None))
    return jax.shard_map(body, mesh=mesh, in_specs=in_specs, out_specs=out_specs, check_vma=False)
```

profile of v0, /device:TPU:1, one launch (start us, length us, event | category | flops | bytes accessed | tf_op | source)
XLA Modules:
  0.0 291.9 jit_solution(17751798194040656294)
XLA Ops:
  7.2 0.7 all-gather.3.cloned.1.call-update
  8.0 0.7 all-gather.5.cloned.1.call-update
  8.7 0.8 convert_reduce_fusion
  9.5 29.7 %psum.7 = f32[8]{0:T(128)S(1)} all-reduce(f32[8]{0:T(128)S(1)} %convert_reduce_fusion), channel_id=1, replica_groups=mesh['grp'=16,'blk'=16] {'blk'}, use_global_device_ids=true, to_apply=%region_1.0 | all-reduce | flops 8 | bytes 64 | tf_op jit(solution)/shard_map/psum | solution.py:55
  39.2 1.4 reshape.103
  40.6 1.3 copy.68
  42.0 1.4 reshape.104
  43.4 1.3 copy.70
  44.9 9.2 %all-gather.3.cloned.1.call-done = bf16[2048,1024]{1,0:T(8,128)(2,1)} async-done(((bf16[128,1024]{1,0:T(8,128)(2,1)}), bf16[2048,1024]{1,0:T(8,128)(2,1)}) %all-gather.3.cloned.1.call-update) | async-done | bytes 4194320 | tf_op jit(solution)/shard_map/all_gather | solution.py:61
  54.1 6.2 %copy.67 = bf16[4,512,1024]{1,2,0:T(8,128)(2,1)} copy(bf16[4,512,1024]{2,1,0:T(8,128)(2,1)} %bitcast.167) | data formatting | bytes 8388608
  60.3 35.5 %all-gather.5.cloned.1.call-done = bf16[2048,1024]{1,0:T(8,128)(2,1)} async-done(((bf16[128,1024]{1,0:T(8,128)(2,1)}), bf16[2048,1024]{1,0:T(8,128)(2,1)}) %all-gather.5.cloned.1.call-update) | async-done | bytes 4194320 | tf_op jit(solution)/shard_map/all_gather | solution.py:62
  95.9 6.2 %copy.66 = bf16[4,512,1024]{1,2,0:T(8,128)(2,1)} copy(bf16[4,512,1024]{2,1,0:T(8,128)(2,1)} %bitcast.168) | data formatting | bytes 8388608
  102.1 28.1 %while.32 = (s32[]{:T(128)}, f32[8,2,128]{2,1,0:T(2,128)S(1)}, f32[8,2,128]{2,1,0:T(2,128)S(1)}, s32[4]{0:T(128)S(1)}, s32[128]{0:T(128)S(1)}, /*index=5*/bf16[4...) while((s32[]{:T(128)}, f32[8,2,128]{2,1,0:T(2,128)S(1)}, ...), condition=%wide.wide.region_6.7_spmd.clone, body=%wide.wide.region_3.6_spmd.clone.sunk | while | flops 546509440 | bytes 15996595 | solution.py:82
  103.4 1.3 constant_dynamic-slice_fusion.11
  104.7 1.3 constant_dynamic-slice_fusion.10
  106.0 1.5 fusion.77
  107.5 1.6 fusion.78
  110.4 1.3 constant_dynamic-slice_fusion.11
  111.7 1.3 constant_dynamic-slice_fusion.10
  113.0 1.5 fusion.77
  114.5 1.6 fusion.78
  117.4 1.3 constant_dynamic-slice_fusion.11
  118.7 1.3 constant_dynamic-slice_fusion.10
  120.0 1.5 fusion.77
  121.5 1.6 fusion.78
  124.5 1.3 constant_dynamic-slice_fusion.11
  125.8 1.3 constant_dynamic-slice_fusion.10
  127.1 1.5 fusion.77
  128.6 1.6 fusion.78
  130.2 43.4 %while.31 = (s32[]{:T(128)}, f32[128,8,2,128]{0,3,2,1:T(8,128)S(1)}, bf16[4,512,2048]{1,2,0:T(8,128)(2,1)}, bf16[4,512,1024]{1,2,0:T(8,128)(2,1)}, s32[4]{0:T(12...) while((s32[]{:T(128)}, ...), condition=%wide.region_8.9_spmd.clone, body=%wide.region_7.8_spmd.clone.sunk | while | flops 1360724608 | bytes 41121456 | solution.py:114
  130.8 0.6 iota_add_fusion.11
  131.6 1.7 constant_dynamic-slice_fusion.9
  133.3 0.8 fusion.70
  134.1 2.5 fusion.71
  136.6 1.4 fusion.73
  138.0 0.6 fusion.72
  138.6 0.8 convolution_bitcast_fusion.3
  139.6 1.5 constant_dynamic-update-slice_fusion.2
  141.7 0.6 iota_add_fusion.11
  142.5 1.7 constant_dynamic-slice_fusion.9
  144.2 0.8 fusion.70
  144.9 2.5 fusion.71
  147.4 1.4 fusion.73
  148.8 0.6 fusion.72
  149.5 0.8 convolution_bitcast_fusion.3
  150.5 1.4 constant_dynamic-update-slice_fusion.2
  152.5 0.6 iota_add_fusion.11
  153.3 1.7 constant_dynamic-slice_fusion.9
  155.0 0.8 fusion.70
  155.7 2.5 fusion.71
  158.3 1.4 fusion.73
  160.3 0.8 convolution_bitcast_fusion.3
  161.3 1.5 constant_dynamic-update-slice_fusion.2
  163.4 0.6 iota_add_fusion.11
  164.1 1.7 constant_dynamic-slice_fusion.9
  165.8 0.8 fusion.70
  166.6 2.5 fusion.71
  169.1 1.4 fusion.73
  171.1 0.8 convolution_bitcast_fusion.3
  172.1 1.5 constant_dynamic-update-slice_fusion.2
  173.6 11.4 %copy.72 = bf16[4,512,2048]{2,1,0:T(8,128)(2,1)} copy(bf16[4,512,2048]{1,2,0:T(8,128)(2,1)} %get-tuple-element.282) | data formatting | bytes 16777216 | tf_op jit(solution)/shard_map/convert_element_type | solution.py:118
  185.1 1.0 copy.85
  186.2 97.4 %reduce-scatter.2.cloned.1.call-done = bf16[128,2048]{1,0:T(8,128)(2,1)} async-done(((bf16[2048,2048]{1,0:T(8,128)(2,1)}), bf16[128,2048]{1,0:T(8,128)(2,1)}) %reduce-scatter.2.cloned.1.call-update) | async-done | bytes 524304 | tf_op jit(solution)/shard_map/reduce_scatter | solution.py:117
  283.5 1.9 fusion.23
  (53 shorter events, 10.4 us)
Async XLA Ops:
  7.2 37.6 %copy-start = (s32[128]{0:T(128)S(1)}, s32[128]{0:T(128)}, u32[]{:S(2)}) copy-start(s32[128]{0:T(128)} %param.13) | copy-start | bytes 1540
  7.2 46.9 %all-gather.3.cloned.1.call-start = ((), (), s32[]{:S(2)}) async-start(), calls=%async_computation.1 | async-start | bytes 4456448 | tf_op jit(solution)/shard_map/all_gather | solution.py:61
  7.9 88.0 %all-gather.5.cloned.1.call-start = ((), (), s32[]{:S(2)}) async-start(), calls=%async_computation.2 | async-start | bytes 4456448 | tf_op jit(solution)/shard_map/all_gather | solution.py:62
  8.7 274.9 %reduce-scatter.2.cloned.1.call-start = ((), (), s32[]{:S(2)}) async-start(), calls=%async_computation.3 | async-start | bytes 8912896 | tf_op jit(solution)/shard_map/reduce_scatter | solution.py:117
Sparse Core Ops, SparseCore 0:
  9.9 44.2 all-gather.2
  56.0 39.8 all-gather.4
  185.2 98.3 reduce-scatter.1
where the time goes:
time: 294 us; the launch traced here: 292 us
  waiting for transfers between devices  144 us (49%)
  local copies, waits for them, and re-layouts  59.9 us (20%)
  matrix products  36.6 us (12%)
  blocking collectives  29.7 us (10%)
  between operations  13.8 us (5%)
  other arithmetic  7.74 us (3%)
    reduce_scatter x1, waiting for transfers between devices, body(): lax.psum_scatter(key_partial_terms.reshape(token_length, 2 * KV_HEAD_COUN...  97.4 us
    all_gather x1, waiting for transfers between devices, body(): lax.all_gather(values, 'blk', axis=0, tiled=True)  35.5 us
    psum x1, blocking collectives, body(): starts = lax.psum(jnp.sum(below, axis=0), 'blk').astype(jnp.int32)  29.7 us
    dynamic_slice x20, local copies, waits for them, and re-layouts, body(): lax.scan(stats_step, (empty_row_stats, empty_row_stats), (key_blocks, val...  21.8 us
    dot_general x8, matrix products, scores(): jnp.einsum('igrd,jgd->grij', output_grad_heads, heads_of_values, preferre...  16.3 us
    unnamed x6, local copies, waits for them, and re-layouts  15.1 us
    convert_element_type x1, local copies, waits for them, and re-layouts, body(): key_partial_terms.reshape(token_length, 2 * KV_HEAD_COUNT * HEAD_SIZE)  11.4 us
    all_gather x1, waiting for transfers between devices, body(): lax.all_gather(keys, 'blk', axis=0, tiled=True)  9.23 us
  transfers between devices with their start and end apart: 3, of which 3 were waited for; matrix products, arithmetic and copies ran while one was open for 5% of the time, Pallas kernels for 0%

commit v1 on v0

v1 whole, which is shorter than its diff:
```python
import math
import jax
import jax.numpy as jnp
from jax import lax
from jax.experimental import pallas as pl
from jax.experimental.pallas import tpu as pltpu
from jax.sharding import PartitionSpec as P

HQ = 16
KV_HEAD_COUNT = 8
HEAD_SIZE = 128
DOCS = 8
BLOCKS = 16
ROWS = 128
SEG_ROWS = 16
IN_ROWS = 3 * ROWS + SEG_ROWS
TILE = 256
TILES = BLOCKS * ROWS // TILE
WIDEST = 5

score_scale = 1.0 / 12.0
cap_value = 50.0
to_cap = score_scale / cap_value
cap_log2 = cap_value * math.log2(math.e)

NT = (((1,), (1,)), ((), ()))
VMEM_LIMIT = 48 * 1024 * 1024


def vmem():
    return pl.BlockSpec(memory_space=pltpu.VMEM)


def pack_kernel(q_ref, k_ref, v_ref, do_ref, seg_ref, out_ref):
    seg = jnp.broadcast_to(seg_ref[...].astype(jnp.float32), (SEG_ROWS, ROWS)).astype(jnp.bfloat16)
    for h in range(HQ):
        kv_ref = k_ref if h % 2 == 0 else v_ref
        g = h // 2
        out_ref[h, 0:ROWS, :] = q_ref[:, h * HEAD_SIZE : (h + 1) * HEAD_SIZE]
        out_ref[h, ROWS : 2 * ROWS, :] = do_ref[:, h * HEAD_SIZE : (h + 1) * HEAD_SIZE]
        out_ref[h, 2 * ROWS : 3 * ROWS, :] = kv_ref[:, g * HEAD_SIZE : (g + 1) * HEAD_SIZE]
        out_ref[h, 3 * ROWS :, :] = seg


def unpack_kernel(in_ref, dq_ref, dk_ref, dv_ref):
    for h in range(HQ):
        out_ref = dk_ref if h % 2 == 0 else dv_ref
        g = h // 2
        dq_ref[:, h * HEAD_SIZE : (h + 1) * HEAD_SIZE] = in_ref[h, 0:ROWS, :]
        out_ref[:, g * HEAD_SIZE : (g + 1) * HEAD_SIZE] = in_ref[h, ROWS : 2 * ROWS, :]


def main_kernel(
    core_ref, in_ref, other_ref, dq_ref, keep_ref, send_ref,
    k_s, v_s, kt_s, first_s, low_s, dk_s, dv_s,
):
    is_k = core_ref[0] == 0
    for b in range(BLOCKS):
        mine = in_ref[b, 2 * ROWS : 3 * ROWS, :]
        theirs = other_ref[b]
        key = jnp.where(is_k, mine, theirs)
        k_s[b * ROWS : (b + 1) * ROWS, :] = key
        v_s[b * ROWS : (b + 1) * ROWS, :] = jnp.where(is_k, theirs, mine)
        kt_s[:, b * ROWS : (b + 1) * ROWS] = key.T
    dk_s[...] = jnp.zeros_like(dk_s)
    dv_s[...] = jnp.zeros_like(dv_s)

    seg = jnp.concatenate(
        [in_ref[b, 3 * ROWS : IN_ROWS, :][:1].astype(jnp.float32) for b in range(BLOCKS)], axis=0
    )
    first = jnp.zeros_like(seg)
    for d in range(1, DOCS):
        below = jnp.where(seg < float(d), 1.0, 0.0)
        start = jnp.sum(jnp.sum(below, axis=1, keepdims=True), axis=0, keepdims=True)
        first = jnp.where(seg == float(d), start, first)
    first = first.astype(jnp.int32)
    first_s[...] = first
    for i in range(TILES):
        low_s[i] = jnp.min(first[2 * i : 2 * i + 1, :]) // TILE

    def one_block(i, low, width):
        keys = width * TILE
        base = pl.multiple_of(low * TILE, TILE)
        q = in_ref[pl.ds(2 * i, 2), 0:ROWS, :].reshape(TILE, HEAD_SIZE)
        do = in_ref[pl.ds(2 * i, 2), ROWS : 2 * ROWS, :].reshape(TILE, HEAD_SIZE)
        start = jnp.concatenate([first_s[pl.ds(2 * i, 1), :], first_s[pl.ds(2 * i + 1, 1), :]], axis=1)
        key_pos = base + lax.broadcasted_iota(jnp.int32, (keys, TILE), 0)
        query_pos = i * TILE + lax.broadcasted_iota(jnp.int32, (1, TILE), 1)
        visible = (key_pos >= start) & (key_pos <= query_pos)
        raw = lax.dot_general(k_s[pl.ds(base, keys), :], q, NT, preferred_element_type=jnp.float32)
        dprob = lax.dot_general(v_s[pl.ds(base, keys), :], do, NT, preferred_element_type=jnp.float32)
        capped = jnp.tanh(raw * to_cap)
        expo = jnp.where(visible, jnp.exp2(capped * cap_log2), 0.0)
        total = jnp.sum(expo, axis=0, keepdims=True)
        inverse = 1.0 / total
        delta = jnp.sum(expo * dprob, axis=0, keepdims=True) * inverse
        prob = expo * inverse
        dscore = prob * (dprob - delta) * (1.0 - capped * capped)
        prob = prob.astype(jnp.bfloat16)
        dscore = dscore.astype(jnp.bfloat16)
        dv_s[pl.ds(base, keys), :] += jnp.dot(prob, do, preferred_element_type=jnp.float32)
        dk_s[pl.ds(base, keys), :] += jnp.dot(dscore, q, preferred_element_type=jnp.float32)
        dq = jnp.dot(kt_s[:, pl.ds(base, keys)], dscore, preferred_element_type=jnp.float32)
        dq = (dq * score_scale).T.astype(jnp.bfloat16)
        dq_ref[pl.ds(2 * i, 2)] = dq.reshape(2, ROWS, HEAD_SIZE)

    @pl.loop(0, TILES)
    def _(i):
        low = low_s[i]
        for width in range(1, WIDEST + 1):

            @pl.when(i - low + 1 == width)
            def _():
                one_block(i, low, width)

    for b in range(BLOCKS):
        dk = (dk_s[b * ROWS : (b + 1) * ROWS, :] * score_scale).astype(jnp.bfloat16)
        dv = dv_s[b * ROWS : (b + 1) * ROWS, :].astype(jnp.bfloat16)
        keep_ref[b] = jnp.where(is_k, dk, dv)
        send_ref[b] = jnp.where(is_k, dv, dk)


def join_kernel(dq_ref, keep_ref, got_ref, out_ref):
    out_ref[:, 0:ROWS, :] = dq_ref[...]
    total = keep_ref[...].astype(jnp.float32) + got_ref[...].astype(jnp.float32)
    out_ref[:, ROWS:, :] = total.astype(jnp.bfloat16)


def call(kernel, out_shape, operands, scratch=(), smem=0):
    return pl.pallas_call(
        kernel,
        out_shape=out_shape,
        in_specs=[pl.BlockSpec(memory_space=pltpu.SMEM)] * smem + [vmem()] * (len(operands) - smem),
        out_specs=jax.tree.map(lambda _: vmem(), out_shape),
        scratch_shapes=list(scratch),
        compiler_params=pltpu.CompilerParams(vmem_limit_bytes=VMEM_LIMIT),
    )(*operands)


def bf16(*shape):
    return jax.ShapeDtypeStruct(shape, jnp.bfloat16)


def body(queries, keys, values, dout, segments):
    swap = [(i, i ^ 1) for i in range(BLOCKS)]
    core = (lax.axis_index("blk") % 2).astype(jnp.int32).reshape(1)
    packed = call(
        pack_kernel,
        bf16(BLOCKS, IN_ROWS, HEAD_SIZE),
        (queries, keys, values, dout, segments.reshape(1, ROWS)),
    )
    mine = lax.all_to_all(packed, "blk", 0, 0, tiled=True)
    other = lax.ppermute(mine[:, 2 * ROWS : 3 * ROWS, :], "blk", swap)
    tokens = BLOCKS * ROWS
    dq, keep, send = call(
        main_kernel,
        (bf16(BLOCKS, ROWS, HEAD_SIZE),) * 3,
        (core, mine, other),
        scratch=(
            pltpu.VMEM((tokens, HEAD_SIZE), jnp.bfloat16),
            pltpu.VMEM((tokens, HEAD_SIZE), jnp.bfloat16),
            pltpu.VMEM((HEAD_SIZE, tokens), jnp.bfloat16),
            pltpu.VMEM((BLOCKS, ROWS), jnp.int32),
            pltpu.SMEM((TILES,), jnp.int32),
            pltpu.VMEM((tokens, HEAD_SIZE), jnp.float32),
            pltpu.VMEM((tokens, HEAD_SIZE), jnp.float32),
        ),
        smem=1,
    )
    got = lax.ppermute(send, "blk", swap)
    joined = call(join_kernel, bf16(BLOCKS, 2 * ROWS, HEAD_SIZE), (dq, keep, got))
    back = lax.all_to_all(joined, "blk", 0, 0, tiled=True)
    return call(
        unpack_kernel,
        (bf16(ROWS, HQ * HEAD_SIZE), bf16(ROWS, KV_HEAD_COUNT * HEAD_SIZE), bf16(ROWS, KV_HEAD_COUNT * HEAD_SIZE)),
        (back,),
    )


def solution(mesh):
    rows = P(("grp", "blk"), None)
    in_specs = (rows, rows, rows, rows, P(("grp", "blk")))
    return jax.shard_map(body, mesh=mesh, in_specs=in_specs, out_specs=(rows, rows, rows), check_vma=False)
```

time: 294 us -> 68.3 us (0.23)
  waiting for transfers between devices: 144 us -> 3.08 us
  local copies, waits for them, and re-layouts: 59.9 us -> 4.67 us
  matrix products: 36.6 us -> 0 us
  blocking collectives: 29.7 us -> 47.5 us
  between operations: 13.8 us -> 0.67 us
  Pallas kernels: 0 us -> 11 us
  other arithmetic: 7.74 us -> 0 us
    reduce_scatter x1 -> x0, waiting for transfers between devices: 97.4 us -> none  [body(): lax.psum_scatter(key_partial_terms.reshape(token_length, 2 * KV_HEAD_COUN...]
    all_to_all x0 -> x2, blocking collectives: none -> 47.5 us  [the longest x1 29.2 us: body(): mine = lax.all_to_all(packed, 'blk', 0, 0, tiled=True)]
    all_gather x2 -> x0, waiting for transfers between devices: 44.8 us -> none  [the longest x1 35.5 us: body(): lax.all_gather(values, 'blk', axis=0, tiled=True)]
    dot_general x28 -> x0, matrix products: 36.6 us -> none  [the longest x8 16.3 us: scores(): jnp.einsum('igrd,jgd->grij', output_grad_heads, heads_of_values, preferre...]
    psum x1 -> x0, blocking collectives: 29.7 us -> none  [body(): starts = lax.psum(jnp.sum(below, axis=0), 'blk').astype(jnp.int32)]
    dynamic_slice x20 -> x0, local copies, waits for them, and re-layouts: 21.8 us -> none  [body(): lax.scan(stats_step, (empty_row_stats, empty_row_stats), (key_blocks, val...]
    convert_element_type x2 -> x0, local copies, waits for them, and re-layouts: 12.4 us -> none  [the longest x1 11.4 us: body(): key_partial_terms.reshape(token_length, 2 * KV_HEAD_COUNT * HEAD_SIZE)]
    pallas_call x0 -> x4, Pallas kernels: none -> 11 us  [call(): pl.pallas_call(kernel, out_shape=out_shape, in_specs=[pl.BlockSpec(memory...]
  transfers between devices with their start and end apart: 3 -> 2, of which waited for: 3 -> 2; matrix products, arithmetic and copies ran while one was open for 5% -> 0% of each run, Pallas kernels for 0% -> 0%
where the time goes in v1:
time: 68.3 us; the launch traced here: 67.9 us
  blocking collectives  47.5 us (70%)
  Pallas kernels  11 us (16%)
  local copies, waits for them, and re-layouts  4.67 us (7%)
  waiting for transfers between devices  3.08 us (5%)
  starting transfers between devices  0.98 us (1%)
    all_to_all x1, blocking collectives, body(): mine = lax.all_to_all(packed, 'blk', 0, 0, tiled=True)  29.2 us
    all_to_all x1, blocking collectives, body(): back = lax.all_to_all(joined, 'blk', 0, 0, tiled=True)  18.3 us
    pallas_call x4, Pallas kernels, call(): pl.pallas_call(kernel, out_shape=out_shape, in_specs=[pl.BlockSpec(memory...  11 us
    unnamed x10, local copies, waits for them, and re-layouts  4.63 us
    ppermute x1, waiting for transfers between devices, body(): got = lax.ppermute(send, 'blk', swap)  1.54 us
    ppermute x1, waiting for transfers between devices, body(): other = lax.ppermute(mine[:, 2 * ROWS:3 * ROWS, :], 'blk', swap)  1.54 us
  transfers between devices with their start and end apart: 2, of which 2 were waited for; matrix products, arithmetic and copies ran while one was open for 0% of the time, Pallas kernels for 0%

profile of v1, /device:TPU:1, one launch (start us, length us, event | category | flops | bytes accessed | tf_op | source)
XLA Modules:
  0.0 67.9 jit_solution(13440841658078270414)
XLA Ops:
  0.6 0.0 copy-start
  0.6 1.0 %copy-done = bf16[128,2048]{1,0:T(8,128)(2,1)S(1)} copy-done((bf16[128,2048]{1,0:T(8,128)(2,1)S(1)}, bf16[128,2048]{1,0:T(8,128)(2,1)}, u32[]{:S(2)}) %copy-start) | copy-done | bytes 524312
  1.7 0.0 copy-start.1
  1.7 1.0 %copy-done.1 = bf16[128,2048]{1,0:T(8,128)(2,1)S(1)} copy-done((bf16[128,2048]{1,0:T(8,128)(2,1)S(1)}, bf16[128,2048]{1,0:T(8,128)(2,1)}, u32[]{:S(2)}) %copy-start.1) | copy-done | bytes 524312
  2.7 0.0 copy-start.2
  2.7 0.9 %copy-done.2 = bf16[128,1024]{1,0:T(8,128)(2,1)S(1)} copy-done((bf16[128,1024]{1,0:T(8,128)(2,1)S(1)}, bf16[128,1024]{1,0:T(8,128)(2,1)}, u32[]{:S(2)}) %copy-start.2) | copy-done | bytes 262168
  3.7 0.0 copy-start.3
  3.7 0.9 %copy-done.3 = bf16[128,1024]{1,0:T(8,128)(2,1)S(1)} copy-done((bf16[128,1024]{1,0:T(8,128)(2,1)S(1)}, bf16[128,1024]{1,0:T(8,128)(2,1)}, u32[]{:S(2)}) %copy-start.3) | copy-done | bytes 262168
  4.6 0.0 copy-start.4
  4.6 0.7 copy-done.4
  5.3 0.3 shard_map.76
  5.6 29.2 %all_to_all.10.in_ref = bf16[16,400,128]{2,1,0:T(8,128)(2,1)S(1)} all-to-all(bf16[16,400,128]{2,1,0:T(8,128)(2,1)S(1)} %shard_map.76), channel_id=1, replica_groups=mesh['grp'=16,'blk'=16] {'blk'}, dimensions={0} | all-to-all | bytes 3276800 | tf_op jit(solution)/shard_map/all_to_all | solution.py:152
  34.8 0.5 collective-permute-start
  35.3 1.5 %collective-permute-done.other_ref = bf16[16,128,128]{2,1,0:T(8,128)(2,1)S(1)} collective-permute-done((bf16[16,128,128]{2,1,0:T(8,128)(2,1)S(1)}, bf16[16,128,128]{2,1,0:T(8,128)(2,1)S(1)}, u32[]{:S(2)}, u32[]{:S(2)}) %collective-permute-start) | collective-permute-done | bytes 524320 | tf_op jit(solution)/shard_map/ppermute | solution.py:153
  36.9 9.3 %shard_map.77 = (bf16[16,128,128]{2,1,0:T(8,128)(2,1)S(1)}, bf16[16,128,128]{2,1,0:T(8,128)(2,1)S(1)}, bf16[16,128,128]{2,1,0:T(8,128)(2,1)S(1)}) custom-call(s32[1]{0:T(128)} %bitcast.core_ref, bf16[16,400,128]{2,1,0:T(8,128)(2,1)S(1)} %all_to_all.10.in_ref, bf16[16,128,128]{2,1,0:T(8,128)(2,1)S(1)} %collective-permute-done.other_ref), custom_call_target="tpu_custom_call" | custom-call | tf_op jit(solution)/shard_map/pallas_call | solution.py:130
  46.2 0.5 collective-permute-start.1
  46.6 1.5 %collective-permute-done.1.got_ref = bf16[16,128,128]{2,1,0:T(8,128)(2,1)S(1)} collective-permute-done((bf16[16,128,128]{2,1,0:T(8,128)(2,1)S(1)}, bf16[16,128,128]{2,1,0:T(8,128)(2,1)S(1)}, u32[]{:S(2)}, u32[]{:S(2)}) %collective-permute-start.1) | collective-permute-done | bytes 524320 | tf_op jit(solution)/shard_map/ppermute | solution.py:170
  48.2 0.2 shard_map.78
  48.3 18.3 %all_to_all.11.in_ref = bf16[16,256,128]{2,1,0:T(8,128)(2,1)S(1)} all-to-all(bf16[16,256,128]{2,1,0:T(8,128)(2,1)S(1)} %shard_map.78), channel_id=1, replica_groups=mesh['grp'=16,'blk'=16] {'blk'}, dimensions={0} | all-to-all | bytes 2097152 | tf_op jit(solution)/shard_map/all_to_all | solution.py:172
  66.6 1.2 %shard_map.79 = (bf16[128,2048]{1,0:T(8,128)(2,1)}, bf16[128,1024]{1,0:T(8,128)(2,1)}, bf16[128,1024]{1,0:T(8,128)(2,1)}) custom-call(bf16[16,256,128]{2,1,0:T(8,128)(2,1)S(1)} %all_to_all.11.in_ref), custom_call_target="tpu_custom_call" | custom-call | tf_op jit(solution)/shard_map/pallas_call | solution.py:130
  (1 shorter events, 0.0 us)
Async XLA Ops:
  0.6 1.0 %copy-start = (bf16[128,2048]{1,0:T(8,128)(2,1)S(1)}, bf16[128,2048]{1,0:T(8,128)(2,1)}, u32[]{:S(2)}) copy-start(bf16[128,2048]{1,0:T(8,128)(2,1)} %q_ref.1) | copy-start | bytes 1572868
  1.7 1.0 %copy-start.1 = (bf16[128,2048]{1,0:T(8,128)(2,1)S(1)}, bf16[128,2048]{1,0:T(8,128)(2,1)}, u32[]{:S(2)}) copy-start(bf16[128,2048]{1,0:T(8,128)(2,1)} %do_ref.1) | copy-start | bytes 1572868
  2.7 0.9 %copy-start.2 = (bf16[128,1024]{1,0:T(8,128)(2,1)S(1)}, bf16[128,1024]{1,0:T(8,128)(2,1)}, u32[]{:S(2)}) copy-start(bf16[128,1024]{1,0:T(8,128)(2,1)} %k_ref.1) | copy-start | bytes 786436
  3.7 0.9 %copy-start.3 = (bf16[128,1024]{1,0:T(8,128)(2,1)S(1)}, bf16[128,1024]{1,0:T(8,128)(2,1)}, u32[]{:S(2)}) copy-start(bf16[128,1024]{1,0:T(8,128)(2,1)} %v_ref.1) | copy-start | bytes 786436
  4.6 0.7 copy-start.4
  34.8 2.1 %collective-permute-start = (bf16[16,128,128]{2,1,0:T(8,128)(2,1)S(1)}, bf16[16,128,128]{2,1,0:T(8,128)(2,1)S(1)}, u32[]{:S(2)}, u32[]{:S(2)}) collective-permute-start(bf16[16,128,128]{2,1,0:T(8,128)(2,1)S(1)} %slice.4), channel_id=1, source_target_pairs={{0,1},{1,0},{2,3},{3,2},{4,5},{5,4},{6,7},{7,6},{8,9},{9,8},{10,11... | collective-permute-start | bytes 1572872 | tf_op jit(solution)/shard_map/ppermute | solution.py:153
  46.2 2.0 %collective-permute-start.1 = (bf16[16,128,128]{2,1,0:T(8,128)(2,1)S(1)}, bf16[16,128,128]{2,1,0:T(8,128)(2,1)S(1)}, u32[]{:S(2)}, u32[]{:S(2)}) collective-permute-start(bf16[16,128,128]{2,1,0:T(8,128)(2,1)S(1)} %get-tuple-element.8), channel_id=1, source_target_pairs={{0,1},{1,0},{2,3},{3,2},{4,5},{5,4},{6,7},{7,6},{8,9},{9,8},{10,11... | collective-permute-start | bytes 1572872 | tf_op jit(solution)/shard_map/ppermute | solution.py:170

commit v2 on v0

v2 whole, which is shorter than its diff:
```python
import math
import jax
import jax.numpy as jnp
from jax import lax
from jax.experimental import pallas as pl
from jax.experimental.pallas import tpu as pltpu
from jax.sharding import PartitionSpec as P

HEAD_SIZE = 128
DOCS = 8
CHIPS = 8
CORES = 2
ROWS = 128
PAIR = CORES * ROWS
SEG_ROWS = 16
DO_AT = PAIR
KV_AT = 2 * PAIR
KV_ROWS = 2 * ROWS + SEG_ROWS
IN_ROWS = KV_AT + KV_ROWS
TOKENS = CHIPS * PAIR
WIDEST = 9

score_scale = 1.0 / 12.0
cap_value = 50.0
to_cap = score_scale / cap_value
cap_log2 = cap_value * math.log2(math.e)

NT = (((1,), (1,)), ((), ()))
VMEM_LIMIT = 32 * 1024 * 1024

ANY = pl.BlockSpec(memory_space=pl.ANY)
HBM = pl.BlockSpec(memory_space=pltpu.HBM)
VMEM = pl.BlockSpec(memory_space=pltpu.VMEM)
SMEM = pl.BlockSpec(memory_space=pltpu.SMEM)


def bf16(*shape):
    return jax.ShapeDtypeStruct(shape, jnp.bfloat16)


def columns(h):
    return pl.ds(h * HEAD_SIZE, HEAD_SIZE)


def run_copies(pairs, sem):
    started = [pltpu.make_async_copy(a, b, sem.at[n]) for n, (a, b) in enumerate(pairs)]
    for copy in started:
        copy.start()
    for copy in started:
        copy.wait()


def pack_kernel(q_ref, k_ref, v_ref, do_ref, seg_ref, out_ref, seg_s, sem):
    pairs = [(seg_ref, seg_s)]
    for m in range(CHIPS):
        for part in range(2):
            at = pl.ds(part * ROWS, ROWS)
            pairs.append((q_ref.at[:, columns(2 * m + part)], out_ref.at[m, at, :]))
            at = pl.ds(DO_AT + part * ROWS, ROWS)
            pairs.append((do_ref.at[:, columns(2 * m + part)], out_ref.at[m, at, :]))
        pairs.append((k_ref.at[:, columns(m)], out_ref.at[m, pl.ds(KV_AT, ROWS), :]))
        pairs.append((v_ref.at[:, columns(m)], out_ref.at[m, pl.ds(KV_AT + ROWS, ROWS), :]))

    run_copies(pairs, sem)
    seg = jnp.broadcast_to(seg_s[...].astype(jnp.float32), (SEG_ROWS, ROWS))
    for m in range(CHIPS):
        out_ref[m, KV_AT + 2 * ROWS :, :] = seg.astype(jnp.bfloat16)


def unpack_kernel(in_ref, dq_ref, dk_ref, dv_ref, sem):
    pairs = []
    for m in range(CHIPS):
        for part in range(2):
            pairs.append((in_ref.at[m, pl.ds(part * ROWS, ROWS), :], dq_ref.at[:, columns(2 * m + part)]))
        pairs.append((in_ref.at[m, pl.ds(PAIR, ROWS), :], dk_ref.at[:, columns(m)]))
        pairs.append((in_ref.at[m, pl.ds(PAIR + ROWS, ROWS), :], dv_ref.at[:, columns(m)]))
    run_copies(pairs, sem)


def main_kernel(
    core_ref, in_ref, other_ref, dq_ref, keep_ref, send_ref,
    k_s, v_s, kt_s, first_s, low_s, dk_s, dv_s, e_s, g_s, dp_s, p_s, ds_s,
):
    core = core_ref[0]
    seg_rows = []
    for n in range(CHIPS):
        for which, ref, at in ((core, in_ref, KV_AT), (1 - core, other_ref, 0)):
            rows = pl.ds(pl.multiple_of(n * PAIR + which * ROWS, ROWS), ROWS)
            key = ref[n, at : at + ROWS, :]
            k_s[rows, :] = key
            v_s[rows, :] = ref[n, at + ROWS : at + 2 * ROWS, :]
            kt_s[:, rows] = key.T
        mine = in_ref[n, KV_AT + 2 * ROWS :, :][:1].astype(jnp.float32)
        theirs = other_ref[n, 2 * ROWS :, :][:1].astype(jnp.float32)
        seg_rows.append((mine, theirs))
    dk_s[...] = jnp.zeros_like(dk_s)
    dv_s[...] = jnp.zeros_like(dv_s)

    mine = jnp.concatenate([a for a, _ in seg_rows], axis=0)
    theirs = jnp.concatenate([b for _, b in seg_rows], axis=0)
    first = jnp.zeros_like(mine)
    for d in range(1, DOCS):
        below = jnp.where(mine < float(d), 1.0, 0.0) + jnp.where(theirs < float(d), 1.0, 0.0)
        start = jnp.sum(jnp.sum(below, axis=1, keepdims=True), axis=0, keepdims=True)
        first = jnp.where(mine == float(d), start, first)
    first = first.astype(jnp.int32)
    first_s[:, 0:ROWS] = first
    first_s[:, ROWS:] = first
    for n in range(CHIPS):
        low_s[n] = jnp.min(first[n : n + 1, :]) // ROWS

    def one_block(n, low, width):
        q = in_ref[n, 0:PAIR, :]
        do = in_ref[n, DO_AT : DO_AT + PAIR, :]
        start = first_s[pl.ds(n, 1), :]
        key_at = lax.broadcasted_iota(jnp.int32, (ROWS, PAIR), 0)
        query_at = lax.broadcasted_iota(jnp.int32, (ROWS, PAIR), 1) % ROWS
        total = jnp.zeros((8, PAIR), jnp.float32)
        delta = jnp.zeros((8, PAIR), jnp.float32)
        for j in range(width):
            rows = pl.ds(pl.multiple_of((low + j) * ROWS, ROWS), ROWS)
            at = pl.ds(j * ROWS, ROWS)
            raw = lax.dot_general(k_s[rows, :], q, NT, preferred_element_type=jnp.float32)
            dprob = lax.dot_general(v_s[rows, :], do, NT, preferred_element_type=jnp.float32)
            capped = jnp.tanh(raw * to_cap)
            expo = jnp.exp2(capped * cap_log2)
            visible = key_at >= start - (low + j) * ROWS
            if j == width - 1:
                visible = visible & (key_at <= query_at)
            expo = jnp.where(visible, expo, 0.0)
            total += jnp.sum(expo.reshape(ROWS // 8, 8, PAIR), axis=0)
            delta += jnp.sum((expo * dprob).reshape(ROWS // 8, 8, PAIR), axis=0)
            e_s[at, :] = expo
            g_s[at, :] = expo * (1.0 - capped * capped)
            dp_s[at, :] = dprob
        inverse = 1.0 / jnp.sum(total, axis=0, keepdims=True)
        delta = jnp.sum(delta, axis=0, keepdims=True) * inverse
        for j in range(width):
            at = pl.ds(j * ROWS, ROWS)
            p_s[at, :] = (e_s[at, :] * inverse).astype(jnp.bfloat16)
            ds_s[at, :] = (g_s[at, :] * ((dp_s[at, :] - delta) * inverse)).astype(jnp.bfloat16)
        keys = width * ROWS
        rows = pl.ds(pl.multiple_of(low * ROWS, ROWS), keys)
        dscore = ds_s[0:keys, :]
        dv_s[rows, :] += jnp.dot(p_s[0:keys, :], do, preferred_element_type=jnp.float32)
        dk_s[rows, :] += jnp.dot(dscore, q, preferred_element_type=jnp.float32)
        dq = jnp.dot(kt_s[:, rows], dscore, preferred_element_type=jnp.float32)
        dq_ref[n] = (dq * score_scale).T.astype(jnp.bfloat16)

    @pl.loop(0, CHIPS)
    def _(n):
        low = low_s[n]
        for width in range(1, WIDEST + 1):

            @pl.when(2 * n + core + 1 - low == width)
            def _():
                one_block(n, low, width)

    for n in range(CHIPS):
        for which, ref in ((core, keep_ref), (1 - core, send_ref)):
            rows = pl.ds(pl.multiple_of(n * PAIR + which * ROWS, ROWS), ROWS)
            ref[n, 0:ROWS, :] = (dk_s[rows, :] * score_scale).astype(jnp.bfloat16)
            ref[n, ROWS:, :] = dv_s[rows, :].astype(jnp.bfloat16)


def join_kernel(dq_ref, keep_ref, got_ref, out_ref):
    out_ref[:, 0:PAIR, :] = dq_ref[...]
    total = keep_ref[...].astype(jnp.float32) + got_ref[...].astype(jnp.float32)
    out_ref[:, PAIR:, :] = total.astype(jnp.bfloat16)


def call(kernel, out_shape, in_specs, out_specs, scratch, operands, flops=0):
    return pl.pallas_call(
        kernel,
        out_shape=out_shape,
        in_specs=in_specs,
        out_specs=out_specs,
        scratch_shapes=scratch,
        cost_estimate=pl.CostEstimate(flops=flops, bytes_accessed=1 << 20, transcendentals=0),
        compiler_params=pltpu.CompilerParams(vmem_limit_bytes=VMEM_LIMIT),
    )(*operands)


def main(core, first, other):
    return call(
        main_kernel,
        (bf16(CHIPS, PAIR, HEAD_SIZE),) * 3,
        [SMEM, VMEM, VMEM], (VMEM,) * 3,
        [
            pltpu.VMEM((TOKENS, HEAD_SIZE), jnp.bfloat16),
            pltpu.VMEM((TOKENS, HEAD_SIZE), jnp.bfloat16),
            pltpu.VMEM((HEAD_SIZE, TOKENS), jnp.bfloat16),
            pltpu.VMEM((CHIPS, PAIR), jnp.int32),
            pltpu.SMEM((CHIPS,), jnp.int32),
            pltpu.VMEM((TOKENS, HEAD_SIZE), jnp.float32),
            pltpu.VMEM((TOKENS, HEAD_SIZE), jnp.float32),
            pltpu.VMEM((WIDEST * ROWS, PAIR), jnp.float32),
            pltpu.VMEM((WIDEST * ROWS, PAIR), jnp.float32),
            pltpu.VMEM((WIDEST * ROWS, PAIR), jnp.float32),
            pltpu.VMEM((WIDEST * ROWS, PAIR), jnp.bfloat16),
            pltpu.VMEM((WIDEST * ROWS, PAIR), jnp.bfloat16),
        ],
        (core, first, other),
        flops=1 << 32,
    )


def body(queries, keys, values, dout, segments):
    swap = [(i, i ^ 1) for i in range(CHIPS * CORES)]
    planes = [[CORES * n + c for n in range(CHIPS)] for c in range(CORES)]
    core = (lax.axis_index("blk") % CORES).astype(jnp.int32).reshape(1)
    packed = call(
        pack_kernel, bf16(CHIPS, IN_ROWS, HEAD_SIZE), [HBM] * 5, VMEM,
        [pltpu.VMEM((1, ROWS), jnp.int32), pltpu.SemaphoreType.DMA((6 * CHIPS + 1,))],
        [
            pltpu.with_memory_space_constraint(a, pltpu.HBM)
            for a in (queries, keys, values, dout, segments.reshape(1, ROWS))
        ],
    )
    first = lax.all_to_all(packed, "blk", 0, 0, tiled=True, axis_index_groups=planes)
    other = lax.ppermute(first[:, KV_AT:, :], "blk", swap)
    dq, keep, send = main(core, first, other)
    got = lax.ppermute(send, "blk", swap)
    joined = call(
        join_kernel, bf16(CHIPS, 2 * PAIR, HEAD_SIZE), [VMEM] * 3, VMEM, [], (dq, keep, got)
    )
    back = lax.all_to_all(joined, "blk", 0, 0, tiled=True, axis_index_groups=planes)
    narrow = bf16(ROWS, CHIPS * HEAD_SIZE)
    return call(
        unpack_kernel, (bf16(ROWS, 2 * CHIPS * HEAD_SIZE), narrow, narrow), [VMEM], (HBM,) * 3,
        [pltpu.SemaphoreType.DMA((4 * CHIPS,))], (back,),
    )


def solution(mesh):
    rows = P(("grp", "blk"), None)
    in_specs = (rows, rows, rows, rows, P(("grp", "blk")))
    return jax.shard_map(body, mesh=mesh, in_specs=in_specs, out_specs=(rows, rows, rows), check_vma=False)
```

time: 294 us -> 62.8 us (0.21)
  waiting for transfers between devices: 144 us -> 3.48 us
  local copies, waits for them, and re-layouts: 59.9 us -> 0.04 us
  matrix products: 36.6 us -> 0 us
  blocking collectives: 29.7 us -> 44.6 us
  between operations: 13.8 us -> 0.67 us
  Pallas kernels: 0 us -> 11.6 us
  other arithmetic: 7.74 us -> 0 us
    reduce_scatter x1 -> x0, waiting for transfers between devices: 97.4 us -> none  [body(): lax.psum_scatter(key_partial_terms.reshape(token_length, 2 * KV_HEAD_COUN...]
    all_gather x2 -> x0, waiting for transfers between devices: 44.8 us -> none  [the longest x1 35.5 us: body(): lax.all_gather(values, 'blk', axis=0, tiled=True)]
    all_to_all x0 -> x2, blocking collectives: none -> 44.6 us  [the longest x1 26.5 us: body(): lax.all_to_all(packed, 'blk', 0, 0, tiled=True, axis_index_groups=planes)]
    dot_general x28 -> x0, matrix products: 36.6 us -> none  [the longest x8 16.3 us: scores(): jnp.einsum('igrd,jgd->grij', output_grad_heads, heads_of_values, preferre...]
    psum x1 -> x0, blocking collectives: 29.7 us -> none  [body(): starts = lax.psum(jnp.sum(below, axis=0), 'blk').astype(jnp.int32)]
    dynamic_slice x20 -> x0, local copies, waits for them, and re-layouts: 21.8 us -> none  [body(): lax.scan(stats_step, (empty_row_stats, empty_row_stats), (key_blocks, val...]
    unnamed x6 -> x0, local copies, waits for them, and re-layouts: 15.1 us -> none
    convert_element_type x2 -> x0, local copies, waits for them, and re-layouts: 12.4 us -> none  [the longest x1 11.4 us: body(): key_partial_terms.reshape(token_length, 2 * KV_HEAD_COUNT * HEAD_SIZE)]
  transfers between devices with their start and end apart: 3 -> 2, of which waited for: 3 -> 2; matrix products, arithmetic and copies ran while one was open for 5% -> 0% of each run, Pallas kernels for 0% -> 0%
where the time goes in v2:
time: 62.8 us; the launch traced here: 62.6 us
  blocking collectives  44.6 us (71%)
  Pallas kernels  11.6 us (18%)
  waiting for transfers between devices  3.48 us (6%)
  starting transfers between devices  2.3 us (4%)
  between operations  0.67 us (1%)
    all_to_all x1, blocking collectives, body(): lax.all_to_all(packed, 'blk', 0, 0, tiled=True, axis_index_groups=planes)  26.5 us
    all_to_all x1, blocking collectives, body(): lax.all_to_all(joined, 'blk', 0, 0, tiled=True, axis_index_groups=planes)  18.1 us
    pallas_call x4, Pallas kernels, call(): pl.pallas_call(kernel, out_shape=out_shape, in_specs=in_specs, out_specs=...  11.6 us
    ppermute x1, starting transfers between devices, body(): other = lax.ppermute(first[:, KV_AT:, :], 'blk', swap)  2.2 us
    ppermute x1, waiting for transfers between devices, body(): got = lax.ppermute(send, 'blk', swap)  1.9 us
    ppermute x1, waiting for transfers between devices, body(): other = lax.ppermute(first[:, KV_AT:, :], 'blk', swap)  1.58 us
  transfers between devices with their start and end apart: 2, of which 2 were waited for; matrix products, arithmetic and copies ran while one was open for 0% of the time, Pallas kernels for 0%

profile of v2, /device:TPU:1, one launch (start us, length us, event | category | flops | bytes accessed | tf_op | source)
XLA Modules:
  0.0 62.6 jit_solution(18094153884765169566)
XLA Ops:
  0.6 1.8 %shard_map.76 = bf16[8,784,128]{2,1,0:T(8,128)(2,1)S(1)} custom-call(bf16[128,2048]{1,0:T(8,128)(2,1)} %q_ref.1, bf16[128,1024]{1,0:T(8,128)(2,1)} %k_ref.1, bf16[128,1024]{1,0:T(8,128)(2,1)} %v_ref.1, bf16[128,2048]{1,0:T(8,128)(2,1)} %do_ref.1, s32[1,128]{1,0:T(1,128)} %bitcast.2), custom_call_target="tpu_custom_call" | custom-call | bytes 1048576 | tf_op jit(solution)/shard_map/pallas_call | solution.py:173
  2.5 26.5 %all_to_all.10.in_ref = bf16[8,784,128]{2,1,0:T(8,128)(2,1)S(1)} all-to-all(bf16[8,784,128]{2,1,0:T(8,128)(2,1)S(1)} %shard_map.76), channel_id=1, replica_groups={{0,2,4,6,8,10,12,14},{1,3,5,7,9,11,13,15},{16,18,20,22,24,26,28,30},{17..., dimensions={0} | all-to-all | bytes 3211264 | tf_op jit(solution)/shard_map/all_to_all | solution.py:220
  29.0 2.2 %collective-permute-start = (bf16[8,272,128]{2,1,0:T(8,128)(2,1)S(1)}, bf16[8,272,128]{2,1,0:T(8,128)(2,1)S(1)}, u32[]{:S(2)}, u32[]{:S(2)}) collective-permute-start(bf16[8,272,128]{2,1,0:T(8,128)(2,1)S(1)} %slice.4), channel_id=1, source_target_pairs={{0,1},{1,0},{2,3},{3,2},{4,5},{5,4},{6,7},{7,6},{8,9},{9,8},{10,11... | collective-permute-start | bytes 1671176 | tf_op jit(solution)/shard_map/ppermute | solution.py:221
  31.2 1.6 %collective-permute-done.other_ref = bf16[8,272,128]{2,1,0:T(8,128)(2,1)S(1)} collective-permute-done((bf16[8,272,128]{2,1,0:T(8,128)(2,1)S(1)}, bf16[8,272,128]{2,1,0:T(8,128)(2,1)S(1)}, u32[]{:S(2)}, u32[]{:S(2)}) %collective-permute-start) | collective-permute-done | bytes 557088 | tf_op jit(solution)/shard_map/ppermute | solution.py:221
  32.8 8.4 %shard_map.77 = (bf16[8,256,128]{2,1,0:T(8,128)(2,1)S(1)}, bf16[8,256,128]{2,1,0:T(8,128)(2,1)S(1)}, bf16[8,256,128]{2,1,0:T(8,128)(2,1)S(1)}) custom-call(s32[1]{0:T(128)} %bitcast.core_ref, bf16[8,784,128]{2,1,0:T(8,128)(2,1)S(1)} %all_to_all.10.in_ref, bf16[8,272,128]{2,1,0:T(8,128)(2,1)S(1)} %collective-permute-done.other_ref), custom_call_target="tpu_custom_call" | custom-call | flops 4294967296 | bytes 1048576 | tf_op jit(solution)/shard_map/pallas_call | solution.py:173
  41.2 0.1 collective-permute-start.1
  41.3 1.9 %collective-permute-done.1.got_ref = bf16[8,256,128]{2,1,0:T(8,128)(2,1)S(1)} collective-permute-done((bf16[8,256,128]{2,1,0:T(8,128)(2,1)S(1)}, bf16[8,256,128]{2,1,0:T(8,128)(2,1)S(1)}, u32[]{:S(2)}, u32[]{:S(2)}) %collective-permute-start.1) | collective-permute-done | bytes 524320 | tf_op jit(solution)/shard_map/ppermute | solution.py:223
  43.2 0.2 shard_map.78
  43.3 18.1 %all_to_all.11.in_ref = bf16[8,512,128]{2,1,0:T(8,128)(2,1)S(1)} all-to-all(bf16[8,512,128]{2,1,0:T(8,128)(2,1)S(1)} %shard_map.78), channel_id=1, replica_groups={{0,2,4,6,8,10,12,14},{1,3,5,7,9,11,13,15},{16,18,20,22,24,26,28,30},{17..., dimensions={0} | all-to-all | bytes 2097152 | tf_op jit(solution)/shard_map/all_to_all | solution.py:227
  61.4 1.2 %shard_map.79 = (bf16[128,2048]{1,0:T(8,128)(2,1)}, bf16[128,1024]{1,0:T(8,128)(2,1)}, bf16[128,1024]{1,0:T(8,128)(2,1)}) custom-call(bf16[8,512,128]{2,1,0:T(8,128)(2,1)S(1)} %all_to_all.11.in_ref), custom_call_target="tpu_custom_call" | custom-call | bytes 1048576 | tf_op jit(solution)/shard_map/pallas_call | solution.py:173
  (1 shorter events, 0.0 us)
Async XLA Ops:
  29.0 3.8 %collective-permute-start = (bf16[8,272,128]{2,1,0:T(8,128)(2,1)S(1)}, bf16[8,272,128]{2,1,0:T(8,128)(2,1)S(1)}, u32[]{:S(2)}, u32[]{:S(2)}) collective-permute-start(bf16[8,272,128]{2,1,0:T(8,128)(2,1)S(1)} %slice.4), channel_id=1, source_target_pairs={{0,1},{1,0},{2,3},{3,2},{4,5},{5,4},{6,7},{7,6},{8,9},{9,8},{10,11... | collective-permute-start | bytes 1671176 | tf_op jit(solution)/shard_map/ppermute | solution.py:221
  41.2 2.0 %collective-permute-start.1 = (bf16[8,256,128]{2,1,0:T(8,128)(2,1)S(1)}, bf16[8,256,128]{2,1,0:T(8,128)(2,1)S(1)}, u32[]{:S(2)}, u32[]{:S(2)}) collective-permute-start(bf16[8,256,128]{2,1,0:T(8,128)(2,1)S(1)} %get-tuple-element.8), channel_id=1, source_target_pairs={{0,1},{1,0},{2,3},{3,2},{4,5},{5,4},{6,7},{7,6},{8,9},{9,8},{10,11... | collective-permute-start | bytes 1572872 | tf_op jit(solution)/shard_map/ppermute | solution.py:223

commit v3 on v2

--- a/solution.py
+++ b/solution.py
@@ -19,6 +19,8 @@
 IN_ROWS = KV_AT + KV_ROWS
 TOKENS = CHIPS * PAIR
 WIDEST = 9
+AHEAD = WIDEST - 1
+AT_ONCE = 2
 
 score_scale = 1.0 / 12.0
 cap_value = 50.0
@@ -26,6 +28,7 @@
 cap_log2 = cap_value * math.log2(math.e)
 
 NT = (((1,), (1,)), ((), ()))
+TN = (((0,), (0,)), ((), ()))
 VMEM_LIMIT = 32 * 1024 * 1024
 
 ANY = pl.BlockSpec(memory_space=pl.ANY)
@@ -40,6 +43,10 @@
 
 def columns(h):
     return pl.ds(h * HEAD_SIZE, HEAD_SIZE)
+
+
+def key_rows(block, blocks=1):
+    return pl.ds(pl.multiple_of((AHEAD + block) * ROWS, ROWS), blocks * ROWS)
 
 
 def run_copies(pairs, sem):
@@ -79,22 +86,22 @@
 
 def main_kernel(
     core_ref, in_ref, other_ref, dq_ref, keep_ref, send_ref,
-    k_s, v_s, kt_s, first_s, low_s, dk_s, dv_s, e_s, g_s, dp_s, p_s, ds_s,
+    k_s, v_s, first_s, width_s, order_s, dk_s, dv_s, *work,
 ):
     core = core_ref[0]
     seg_rows = []
     for n in range(CHIPS):
         for which, ref, at in ((core, in_ref, KV_AT), (1 - core, other_ref, 0)):
-            rows = pl.ds(pl.multiple_of(n * PAIR + which * ROWS, ROWS), ROWS)
-            key = ref[n, at : at + ROWS, :]
-            k_s[rows, :] = key
+            rows = key_rows(2 * n + which)
+            k_s[rows, :] = ref[n, at : at + ROWS, :]
             v_s[rows, :] = ref[n, at + ROWS : at + 2 * ROWS, :]
-            kt_s[:, rows] = key.T
         mine = in_ref[n, KV_AT + 2 * ROWS :, :][:1].astype(jnp.float32)
         theirs = other_ref[n, 2 * ROWS :, :][:1].astype(jnp.float32)
         seg_rows.append((mine, theirs))
-    dk_s[...] = jnp.zeros_like(dk_s)
-    dv_s[...] = jnp.zeros_like(dv_s)
+    k_s[0 : AHEAD * ROWS, :] = jnp.zeros((AHEAD * ROWS, HEAD_SIZE), jnp.bfloat16)
+    v_s[0 : AHEAD * ROWS, :] = jnp.zeros((AHEAD * ROWS, HEAD_SIZE), jnp.bfloat16)
+    dk_s[AHEAD * ROWS :, :] = jnp.zeros((TOKENS, HEAD_SIZE), jnp.float32)
+    dv_s[AHEAD * ROWS :, :] = jnp.zeros((TOKENS, HEAD_SIZE), jnp.float32)
 
     mine = jnp.concatenate([a for a, _ in seg_rows], axis=0)
     theirs = jnp.concatenate([b for _, b in seg_rows], axis=0)
@@ -106,59 +113,84 @@
     first = first.astype(jnp.int32)
     first_s[:, 0:ROWS] = first
     first_s[:, ROWS:] = first
+
+    widths = [2 * n + core + 1 - jnp.min(first[n : n + 1, :]) // ROWS for n in range(CHIPS)]
     for n in range(CHIPS):
-        low_s[n] = jnp.min(first[n : n + 1, :]) // ROWS
-
-    def one_block(n, low, width):
-        q = in_ref[n, 0:PAIR, :]
-        do = in_ref[n, DO_AT : DO_AT + PAIR, :]
-        start = first_s[pl.ds(n, 1), :]
+        before = [widths[m] <= widths[n] if m < n else widths[m] < widths[n] for m in range(CHIPS) if m != n]
+        rank = sum(x.astype(jnp.int32) for x in before)
+        order_s[rank] = n
+        width_s[rank] = widths[n]
+
+    def tiles_at_once(first_at, width):
+        keys = width * ROWS
+        tiles = [order_s[first_at + u] for u in range(AT_ONCE)]
+        low = [2 * n + core + 1 - width for n in tiles]
+        q = [in_ref[n, 0:PAIR, :] for n in tiles]
+        do = [in_ref[n, DO_AT : DO_AT + PAIR, :] for n in tiles]
+        start = [first_s[pl.ds(n, 1), :] for n in tiles]
         key_at = lax.broadcasted_iota(jnp.int32, (ROWS, PAIR), 0)
         query_at = lax.broadcasted_iota(jnp.int32, (ROWS, PAIR), 1) % ROWS
-        total = jnp.zeros((8, PAIR), jnp.float32)
-        delta = jnp.zeros((8, PAIR), jnp.float32)
-        for j in range(width):
-            rows = pl.ds(pl.multiple_of((low + j) * ROWS, ROWS), ROWS)
-            at = pl.ds(j * ROWS, ROWS)
-            raw = lax.dot_general(k_s[rows, :], q, NT, preferred_element_type=jnp.float32)
-            dprob = lax.dot_general(v_s[rows, :], do, NT, preferred_element_type=jnp.float32)
-            capped = jnp.tanh(raw * to_cap)
-            expo = jnp.exp2(capped * cap_log2)
-            visible = key_at >= start - (low + j) * ROWS
-            if j == width - 1:
-                visible = visible & (key_at <= query_at)
-            expo = jnp.where(visible, expo, 0.0)
-            total += jnp.sum(expo.reshape(ROWS // 8, 8, PAIR), axis=0)
-            delta += jnp.sum((expo * dprob).reshape(ROWS // 8, 8, PAIR), axis=0)
-            e_s[at, :] = expo
-            g_s[at, :] = expo * (1.0 - capped * capped)
-            dp_s[at, :] = dprob
-        inverse = 1.0 / jnp.sum(total, axis=0, keepdims=True)
-        delta = jnp.sum(delta, axis=0, keepdims=True) * inverse
+        total = [jnp.zeros((8, PAIR), jnp.float32) for _ in tiles]
+        delta = [jnp.zeros((8, PAIR), jnp.float32) for _ in tiles]
         for j in range(width):
             at = pl.ds(j * ROWS, ROWS)
-            p_s[at, :] = (e_s[at, :] * inverse).astype(jnp.bfloat16)
-            ds_s[at, :] = (g_s[at, :] * ((dp_s[at, :] - delta) * inverse)).astype(jnp.bfloat16)
-        keys = width * ROWS
-        rows = pl.ds(pl.multiple_of(low * ROWS, ROWS), keys)
-        dscore = ds_s[0:keys, :]
-        dv_s[rows, :] += jnp.dot(p_s[0:keys, :], do, preferred_element_type=jnp.float32)
-        dk_s[rows, :] += jnp.dot(dscore, q, preferred_element_type=jnp.float32)
-        dq = jnp.dot(kt_s[:, rows], dscore, preferred_element_type=jnp.float32)
-        dq_ref[n] = (dq * score_scale).T.astype(jnp.bfloat16)
-
-    @pl.loop(0, CHIPS)
-    def _(n):
-        low = low_s[n]
-        for width in range(1, WIDEST + 1):
-
-            @pl.when(2 * n + core + 1 - low == width)
+            for u in range(AT_ONCE):
+                e_s, g_s, dp_s, _, _ = work[5 * u : 5 * u + 5]
+                rows = key_rows(low[u] + j)
+                raw = lax.dot_general(k_s[rows, :], q[u], NT, preferred_element_type=jnp.float32)
+                dprob = lax.dot_general(v_s[rows, :], do[u], NT, preferred_element_type=jnp.float32)
+                capped = jnp.tanh(raw * to_cap)
+                expo = jnp.exp2(capped * cap_log2)
+                visible = key_at >= start[u] - (low[u] + j) * ROWS
+                if j == width - 1:
+                    visible = visible & (key_at <= query_at)
+                expo = jnp.where(visible, expo, 0.0)
+                total[u] += jnp.sum(expo.reshape(ROWS // 8, 8, PAIR), axis=0)
+                delta[u] += jnp.sum((expo * dprob).reshape(ROWS // 8, 8, PAIR), axis=0)
+                e_s[at, :] = expo
+                g_s[at, :] = expo * (1.0 - capped * capped)
+                dp_s[at, :] = dprob
+        inverse = [1.0 / jnp.sum(x, axis=0, keepdims=True) for x in total]
+        delta = [jnp.sum(x, axis=0, keepdims=True) * y for x, y in zip(delta, inverse)]
+        for u in range(AT_ONCE):
+            e_s, g_s, dp_s, p_s, ds_s = work[5 * u : 5 * u + 5]
+            for j in range(width):
+                at = pl.ds(j * ROWS, ROWS)
+                p_s[at, :] = (e_s[at, :] * inverse[u]).astype(jnp.bfloat16)
+                ds_s[at, :] = (g_s[at, :] * ((dp_s[at, :] - delta[u]) * inverse[u])).astype(jnp.bfloat16)
+        for u in range(AT_ONCE):
+            _, _, _, p_s, ds_s = work[5 * u : 5 * u + 5]
+            rows = key_rows(low[u], width)
+            dscore = ds_s[0:keys, :]
+            dv_s[rows, :] += jnp.dot(p_s[0:keys, :], do[u], preferred_element_type=jnp.float32)
+            dk_s[rows, :] += jnp.dot(dscore, q[u], preferred_element_type=jnp.float32)
+            dq = lax.dot_general(dscore, k_s[rows, :], TN, preferred_element_type=jnp.float32)
+            dq_ref[tiles[u]] = (dq * score_scale).astype(jnp.bfloat16)
+
+    @pl.loop(0, CHIPS // AT_ONCE)
+    def _(group):
+        first_at = group * AT_ONCE
+        widest = width_s[first_at + AT_ONCE - 1]
+
+        def choose(least, most):
+            if least == most:
+                tiles_at_once(first_at, least)
+                return
+            middle = (least + most) // 2
+
+            @pl.when(widest <= middle)
             def _():
-                one_block(n, low, width)
+                choose(least, middle)
+
+            @pl.when(widest > middle)
+            def _():
+                choose(middle + 1, most)
+
+        choose(1, WIDEST)
 
     for n in range(CHIPS):
         for which, ref in ((core, keep_ref), (1 - core, send_ref)):
-            rows = pl.ds(pl.multiple_of(n * PAIR + which * ROWS, ROWS), ROWS)
+            rows = key_rows(2 * n + which)
             ref[n, 0:ROWS, :] = (dk_s[rows, :] * score_scale).astype(jnp.bfloat16)
             ref[n, ROWS:, :] = dv_s[rows, :].astype(jnp.bfloat16)
 
@@ -182,24 +214,29 @@
 
 
 def main(core, first, other):
+    rows = (AHEAD * ROWS) + TOKENS
+    seen = (WIDEST * ROWS, PAIR)
     return call(
         main_kernel,
         (bf16(CHIPS, PAIR, HEAD_SIZE),) * 3,
         [SMEM, VMEM, VMEM], (VMEM,) * 3,
         [
-            pltpu.VMEM((TOKENS, HEAD_SIZE), jnp.bfloat16),
-            pltpu.VMEM((TOKENS, HEAD_SIZE), jnp.bfloat16),
-            pltpu.VMEM((HEAD_SIZE, TOKENS), jnp.bfloat16),
+            pltpu.VMEM((rows, HEAD_SIZE), jnp.bfloat16),
+            pltpu.VMEM((rows, HEAD_SIZE), jnp.bfloat16),
             pltpu.VMEM((CHIPS, PAIR), jnp.int32),
             pltpu.SMEM((CHIPS,), jnp.int32),
-            pltpu.VMEM((TOKENS, HEAD_SIZE), jnp.float32),
-            pltpu.VMEM((TOKENS, HEAD_SIZE), jnp.float32),
-            pltpu.VMEM((WIDEST * ROWS, PAIR), jnp.float32),
-            pltpu.VMEM((WIDEST * ROWS, PAIR), jnp.float32),
-            pltpu.VMEM((WIDEST * ROWS, PAIR), jnp.float32),
-            pltpu.VMEM((WIDEST * ROWS, PAIR), jnp.bfloat16),
-            pltpu.VMEM((WIDEST * ROWS, PAIR), jnp.bfloat16),
-        ],
+            pltpu.SMEM((CHIPS,), jnp.int32),
+            pltpu.VMEM((rows, HEAD_SIZE), jnp.float32),
+            pltpu.VMEM((rows, HEAD_SIZE), jnp.float32),
+        ]
+        + [
+            pltpu.VMEM(seen, jnp.float32),
+            pltpu.VMEM(seen, jnp.float32),
+            pltpu.VMEM(seen, jnp.float32),
+            pltpu.VMEM(seen, jnp.bfloat16),
+            pltpu.VMEM(seen, jnp.bfloat16),
+        ]
+        * AT_ONCE,
         (core, first, other),
         flops=1 << 32,
     )

time: 62.8 us -> 61.7 us (0.982)
  Pallas kernels: 11.6 us -> 9.6 us
  starting transfers between devices: 2.3 us -> 3.53 us
    pallas_call x4, Pallas kernels: 11.6 us -> 9.6 us  [call(): pl.pallas_call(kernel, out_shape=out_shape, in_specs=in_specs, out_specs=...]
    ppermute x1, starting transfers between devices: 0.09 us -> 1.33 us  [body(): got = lax.ppermute(send, 'blk', swap)]
where the time goes in v3:
time: 61.7 us; the launch traced here: 61.3 us
  blocking collectives  44.3 us (72%)
  Pallas kernels  9.6 us (16%)
  starting transfers between devices  3.53 us (6%)
  waiting for transfers between devices  3.12 us (5%)
  between operations  0.66 us (1%)
    all_to_all x1, blocking collectives, body(): lax.all_to_all(packed, 'blk', 0, 0, tiled=True, axis_index_groups=planes)  26.5 us
    all_to_all x1, blocking collectives, body(): lax.all_to_all(joined, 'blk', 0, 0, tiled=True, axis_index_groups=planes)  17.8 us
    pallas_call x4, Pallas kernels, call(): pl.pallas_call(kernel, out_shape=out_shape, in_specs=in_specs, out_specs=...  9.6 us
    ppermute x1, starting transfers between devices, body(): other = lax.ppermute(first[:, KV_AT:, :], 'blk', swap)  2.2 us
    ppermute x1, waiting for transfers between devices, body(): other = lax.ppermute(first[:, KV_AT:, :], 'blk', swap)  1.58 us
    ppermute x1, waiting for transfers between devices, body(): got = lax.ppermute(send, 'blk', swap)  1.54 us
    ppermute x1, starting transfers between devices, body(): got = lax.ppermute(send, 'blk', swap)  1.33 us
  transfers between devices with their start and end apart: 2, of which 2 were waited for; matrix products, arithmetic and copies ran while one was open for 0% of the time, Pallas kernels for 0%

profile of v3, /device:TPU:1, one launch (start us, length us, event | category | flops | bytes accessed | tf_op | source)
XLA Modules:
  0.0 61.3 jit_solution(10247017561952613680)
XLA Ops:
  0.6 1.8 %shard_map.76 = bf16[8,784,128]{2,1,0:T(8,128)(2,1)S(1)} custom-call(bf16[128,2048]{1,0:T(8,128)(2,1)} %q_ref.1, bf16[128,1024]{1,0:T(8,128)(2,1)} %k_ref.1, bf16[128,1024]{1,0:T(8,128)(2,1)} %v_ref.1, bf16[128,2048]{1,0:T(8,128)(2,1)} %do_ref.1, s32[1,128]{1,0:T(1,128)} %bitcast.2), custom_call_target="tpu_custom_call" | custom-call | bytes 1048576 | tf_op jit(solution)/shard_map/pallas_call | solution.py:205
  2.5 26.5 %all_to_all.10.in_ref = bf16[8,784,128]{2,1,0:T(8,128)(2,1)S(1)} all-to-all(bf16[8,784,128]{2,1,0:T(8,128)(2,1)S(1)} %shard_map.76), channel_id=1, replica_groups={{0,2,4,6,8,10,12,14},{1,3,5,7,9,11,13,15},{16,18,20,22,24,26,28,30},{17..., dimensions={0} | all-to-all | bytes 3211264 | tf_op jit(solution)/shard_map/all_to_all | solution.py:257
  29.0 2.2 %collective-permute-start = (bf16[8,272,128]{2,1,0:T(8,128)(2,1)S(1)}, bf16[8,272,128]{2,1,0:T(8,128)(2,1)S(1)}, u32[]{:S(2)}, u32[]{:S(2)}) collective-permute-start(bf16[8,272,128]{2,1,0:T(8,128)(2,1)S(1)} %slice.4), channel_id=1, source_target_pairs={{0,1},{1,0},{2,3},{3,2},{4,5},{5,4},{6,7},{7,6},{8,9},{9,8},{10,11... | collective-permute-start | bytes 1671176 | tf_op jit(solution)/shard_map/ppermute | solution.py:258
  31.2 1.6 %collective-permute-done.other_ref = bf16[8,272,128]{2,1,0:T(8,128)(2,1)S(1)} collective-permute-done((bf16[8,272,128]{2,1,0:T(8,128)(2,1)S(1)}, bf16[8,272,128]{2,1,0:T(8,128)(2,1)S(1)}, u32[]{:S(2)}, u32[]{:S(2)}) %collective-permute-start) | collective-permute-done | bytes 557088 | tf_op jit(solution)/shard_map/ppermute | solution.py:258
  32.8 6.4 %shard_map.77 = (bf16[8,256,128]{2,1,0:T(8,128)(2,1)S(1)}, bf16[8,256,128]{2,1,0:T(8,128)(2,1)S(1)}, bf16[8,256,128]{2,1,0:T(8,128)(2,1)S(1)}) custom-call(s32[1]{0:T(128)} %bitcast.core_ref, bf16[8,784,128]{2,1,0:T(8,128)(2,1)S(1)} %all_to_all.10.in_ref, bf16[8,272,128]{2,1,0:T(8,128)(2,1)S(1)} %collective-permute-done.other_ref), custom_call_target="tpu_custom_call" | custom-call | flops 4294967296 | bytes 1048576 | tf_op jit(solution)/shard_map/pallas_call | solution.py:205
  39.2 1.3 %collective-permute-start.1 = (bf16[8,256,128]{2,1,0:T(8,128)(2,1)S(1)}, bf16[8,256,128]{2,1,0:T(8,128)(2,1)S(1)}, u32[]{:S(2)}, u32[]{:S(2)}) collective-permute-start(bf16[8,256,128]{2,1,0:T(8,128)(2,1)S(1)} %get-tuple-element.8), channel_id=1, source_target_pairs={{0,1},{1,0},{2,3},{3,2},{4,5},{5,4},{6,7},{7,6},{8,9},{9,8},{10,11... | collective-permute-start | bytes 1572872 | tf_op jit(solution)/shard_map/ppermute | solution.py:260
  40.5 1.5 %collective-permute-done.1.got_ref = bf16[8,256,128]{2,1,0:T(8,128)(2,1)S(1)} collective-permute-done((bf16[8,256,128]{2,1,0:T(8,128)(2,1)S(1)}, bf16[8,256,128]{2,1,0:T(8,128)(2,1)S(1)}, u32[]{:S(2)}, u32[]{:S(2)}) %collective-permute-start.1) | collective-permute-done | bytes 524320 | tf_op jit(solution)/shard_map/ppermute | solution.py:260
  42.1 0.2 shard_map.78
  42.2 17.8 %all_to_all.11.in_ref = bf16[8,512,128]{2,1,0:T(8,128)(2,1)S(1)} all-to-all(bf16[8,512,128]{2,1,0:T(8,128)(2,1)S(1)} %shard_map.78), channel_id=1, replica_groups={{0,2,4,6,8,10,12,14},{1,3,5,7,9,11,13,15},{16,18,20,22,24,26,28,30},{17..., dimensions={0} | all-to-all | bytes 2097152 | tf_op jit(solution)/shard_map/all_to_all | solution.py:264
  60.0 1.2 %shard_map.79 = (bf16[128,2048]{1,0:T(8,128)(2,1)}, bf16[128,1024]{1,0:T(8,128)(2,1)}, bf16[128,1024]{1,0:T(8,128)(2,1)}) custom-call(bf16[8,512,128]{2,1,0:T(8,128)(2,1)S(1)} %all_to_all.11.in_ref), custom_call_target="tpu_custom_call" | custom-call | bytes 1048576 | tf_op jit(solution)/shard_map/pallas_call | solution.py:205
  (1 shorter events, 0.0 us)
Async XLA Ops:
  29.0 3.8 %collective-permute-start = (bf16[8,272,128]{2,1,0:T(8,128)(2,1)S(1)}, bf16[8,272,128]{2,1,0:T(8,128)(2,1)S(1)}, u32[]{:S(2)}, u32[]{:S(2)}) collective-permute-start(bf16[8,272,128]{2,1,0:T(8,128)(2,1)S(1)} %slice.4), channel_id=1, source_target_pairs={{0,1},{1,0},{2,3},{3,2},{4,5},{5,4},{6,7},{7,6},{8,9},{9,8},{10,11... | collective-permute-start | bytes 1671176 | tf_op jit(solution)/shard_map/ppermute | solution.py:258
  39.2 2.9 %collective-permute-start.1 = (bf16[8,256,128]{2,1,0:T(8,128)(2,1)S(1)}, bf16[8,256,128]{2,1,0:T(8,128)(2,1)S(1)}, u32[]{:S(2)}, u32[]{:S(2)}) collective-permute-start(bf16[8,256,128]{2,1,0:T(8,128)(2,1)S(1)} %get-tuple-element.8), channel_id=1, source_target_pairs={{0,1},{1,0},{2,3},{3,2},{4,5},{5,4},{6,7},{7,6},{8,9},{9,8},{10,11... | collective-permute-start | bytes 1572872 | tf_op jit(solution)/shard_map/ppermute | solution.py:260

commit v4 on v3

v4 whole, which is shorter than its diff:
```python
import functools
import math
import jax
import jax.numpy as jnp
from jax import lax
from jax.experimental import pallas as pl
from jax.experimental.pallas import tpu as pltpu
from jax.sharding import PartitionSpec as P

HEAD_SIZE = 128
DOCS = 8
CHIPS = 8
CORES = 2
ROWS = 128
PAIR = CORES * ROWS
SEG_ROWS = 16
DO_AT = PAIR
KV_AT = 2 * PAIR
KV_ROWS = 2 * ROWS + SEG_ROWS
IN_ROWS = KV_AT + KV_ROWS
TOKENS = CHIPS * PAIR
WIDEST = 9
REACH = 4
AT_ONCE = 2

score_scale = 1.0 / 12.0
cap_value = 50.0
to_cap = score_scale / cap_value
cap_log2 = cap_value * math.log2(math.e)

NT = (((1,), (1,)), ((), ()))
TN = (((0,), (0,)), ((), ()))
VMEM_LIMIT = 32 * 1024 * 1024

ANY = pl.BlockSpec(memory_space=pl.ANY)
HBM = pl.BlockSpec(memory_space=pltpu.HBM)
VMEM = pl.BlockSpec(memory_space=pltpu.VMEM)
SMEM = pl.BlockSpec(memory_space=pltpu.SMEM)


def bf16(*shape):
    return jax.ShapeDtypeStruct(shape, jnp.bfloat16)


def columns(h):
    return pl.ds(h * HEAD_SIZE, HEAD_SIZE)


def pack_kernel(q_ref, k_ref, v_ref, do_ref, seg_ref, out_ref, q_s, k_s, v_s, do_s, seg_s, sem):
    held = (q_s, do_s, k_s, v_s, seg_s)
    copies = [
        pltpu.make_async_copy(a, b, sem.at[n])
        for n, (a, b) in enumerate(zip((q_ref, do_ref, k_ref, v_ref, seg_ref), held))
    ]
    for copy in copies:
        copy.start()
    for copy, ref, at in zip(copies, held, (0, DO_AT)):
        copy.wait()
        for m in range(CHIPS):
            for part in range(2):
                out_ref[m, at + part * ROWS : at + (part + 1) * ROWS, :] = ref[:, columns(2 * m + part)]
    for copy, ref, at in zip(copies[2:], held[2:], (KV_AT, KV_AT + ROWS)):
        copy.wait()
        for m in range(CHIPS):
            out_ref[m, at : at + ROWS, :] = ref[:, columns(m)]
    copies[-1].wait()
    seg = jnp.broadcast_to(seg_s[...].astype(jnp.float32), (SEG_ROWS, ROWS))
    for m in range(CHIPS):
        out_ref[m, KV_AT + 2 * ROWS :, :] = seg.astype(jnp.bfloat16)


def unpack_kernel(in_ref, dq_ref, dk_ref, dv_ref, dq_s, dk_s, dv_s, sem):
    started = []

    def send(held, out):
        started.append(pltpu.make_async_copy(held, out, sem.at[len(started)]))
        started[-1].start()

    for m in range(CHIPS):
        for part in range(2):
            dq_s[:, columns(2 * m + part)] = in_ref[m, part * ROWS : (part + 1) * ROWS, :]
    send(dq_s, dq_ref)
    for held, out, at in ((dk_s, dk_ref, PAIR), (dv_s, dv_ref, PAIR + ROWS)):
        for m in range(CHIPS):
            held[:, columns(m)] = in_ref[m, at : at + ROWS, :]
        send(held, out)
    for copy in started:
        copy.wait()


def seen_blocks(n, core, width, in_ref, other_ref):
    for i in range(width):
        if i % 2 == 0:
            chip, ref, at = jnp.maximum(n - i // 2, 0), in_ref, KV_AT
        else:
            chip, ref, at = jnp.maximum(n - (i + 1) // 2 + core, 0), other_ref, 0
        yield i, 2 * n + core - i, chip, ref.at[chip, pl.ds(at, ROWS)], ref.at[chip, pl.ds(at + ROWS, ROWS)]


def by_width(width, case):
    def choose(least, most):
        if least == most:
            case(least)
            return
        middle = (least + most) // 2

        @pl.when(width <= middle)
        def _():
            choose(least, middle)

        @pl.when(width > middle)
        def _():
            choose(middle + 1, most)

    choose(1, WIDEST)


def main_kernel(
    core_ref, in_ref, other_ref, dq_ref, keep_ref, send_ref, order_ref, width_ref, first_s, *work
):
    core = core_ref[0]
    dk_s, dv_s, work = work[0:2], work[2:4], work[4:]
    for sum_s in (*dk_s, *dv_s):
        sum_s[REACH : REACH + CHIPS] = jnp.zeros((CHIPS, ROWS, HEAD_SIZE), jnp.float32)

    mine = jnp.concatenate(
        [in_ref[n, KV_AT + 2 * ROWS :, :][:1].astype(jnp.float32) for n in range(CHIPS)], axis=0
    )
    theirs = jnp.concatenate([other_ref[n, 2 * ROWS :, :][:1].astype(jnp.float32) for n in range(CHIPS)], axis=0)
    first = jnp.zeros_like(mine)
    for d in range(1, DOCS):
        below = jnp.where(mine < float(d), 1.0, 0.0) + jnp.where(theirs < float(d), 1.0, 0.0)
        start = jnp.sum(jnp.sum(below, axis=1, keepdims=True), axis=0, keepdims=True)
        first = jnp.where(mine == float(d), start, first)
    first = first.astype(jnp.int32)
    first_s[:, 0:ROWS] = first
    first_s[:, ROWS:] = first

    widths = [2 * n + core + 1 - jnp.min(first[n : n + 1, :]) // ROWS for n in range(CHIPS)]
    for n in range(CHIPS):
        before = [widths[m] <= widths[n] if m < n else widths[m] < widths[n] for m in range(CHIPS) if m != n]
        rank = sum(x.astype(jnp.int32) for x in before)
        order_ref[rank] = n
        width_ref[rank] = widths[n]

    def tiles_at_once(first_at, width):
        tiles = [order_ref[first_at + u] for u in range(AT_ONCE)]
        q = [in_ref[n, 0:PAIR, :] for n in tiles]
        do = [in_ref[n, DO_AT : DO_AT + PAIR, :] for n in tiles]
        start = [first_s[pl.ds(n, 1), :] for n in tiles]
        seen = [list(seen_blocks(n, core, width, in_ref, other_ref)) for n in tiles]
        key_at = lax.broadcasted_iota(jnp.int32, (ROWS, PAIR), 0)
        query_at = lax.broadcasted_iota(jnp.int32, (ROWS, PAIR), 1) % ROWS
        total = [jnp.zeros((8, PAIR), jnp.float32) for _ in tiles]
        delta = [jnp.zeros((8, PAIR), jnp.float32) for _ in tiles]
        for j in range(width):
            at = pl.ds(j * ROWS, ROWS)
            for u in range(AT_ONCE):
                e_s, g_s, dp_s = work[3 * u : 3 * u + 3]
                _, block, _, k, v = seen[u][j]
                raw = lax.dot_general(k[...], q[u], NT, preferred_element_type=jnp.float32)
                dprob = lax.dot_general(v[...], do[u], NT, preferred_element_type=jnp.float32)
                capped = jnp.tanh(raw * to_cap)
                expo = jnp.exp2(capped * cap_log2)
                visible = key_at >= start[u] - block * ROWS
                if j == 0:
                    visible = visible & (key_at <= query_at)
                expo = jnp.where(visible, expo, 0.0)
                total[u] += jnp.sum(expo.reshape(ROWS // 8, 8, PAIR), axis=0)
                delta[u] += jnp.sum((expo * dprob).reshape(ROWS // 8, 8, PAIR), axis=0)
                e_s[at, :] = expo
                g_s[at, :] = 1.0 - capped * capped
                dp_s[at, :] = dprob
        dscores = [[] for _ in tiles]
        inverse = [1.0 / jnp.sum(x, axis=0, keepdims=True) for x in total]
        delta = [jnp.sum(x, axis=0, keepdims=True) * y for x, y in zip(delta, inverse)]
        for u in range(AT_ONCE):
            e_s, g_s, dp_s = work[3 * u : 3 * u + 3]
            for j in range(width):
                at = pl.ds(j * ROWS, ROWS)
                prob = e_s[at, :] * inverse[u]
                low = prob.astype(jnp.bfloat16)
                dscore = (prob * (dp_s[at, :] - delta[u]) * g_s[at, :]).astype(jnp.bfloat16)
                which = j % 2
                place = pl.ds(tiles[u] + (core if which else 0), REACH + 1)
                place = REACH - (j + 1) // 2, place
                dv_s[which].at[place[1]][place[0]] += jnp.dot(low, do[u], preferred_element_type=jnp.float32)
                dk_s[which].at[place[1]][place[0]] += jnp.dot(dscore, q[u], preferred_element_type=jnp.float32)
                dscores[u].append(dscore)
        for u in range(AT_ONCE):
            keys = jnp.concatenate([x[3][...] for x in seen[u]], axis=0)
            dscore = jnp.concatenate(dscores[u], axis=0)
            dq = lax.dot_general(dscore, keys, TN, preferred_element_type=jnp.float32)
            dq_ref[tiles[u]] = (dq * score_scale).astype(jnp.bfloat16)

    @pl.loop(0, CHIPS // AT_ONCE)
    def _(group):
        first_at = group * AT_ONCE
        by_width(width_ref[first_at + AT_ONCE - 1], functools.partial(tiles_at_once, first_at))

    for ref, dk, dv in zip((keep_ref, send_ref), dk_s, dv_s):
        ref[:, 0:ROWS, :] = (dk[REACH : REACH + CHIPS] * score_scale).astype(jnp.bfloat16)
        ref[:, ROWS:, :] = dv[REACH : REACH + CHIPS].astype(jnp.bfloat16)


def join_kernel(dq_ref, keep_ref, got_ref, out_ref):
    out_ref[:, 0:PAIR, :] = dq_ref[...]
    total = keep_ref[...].astype(jnp.float32) + got_ref[...].astype(jnp.float32)
    out_ref[:, PAIR:, :] = total.astype(jnp.bfloat16)


def call(kernel, out_shape, in_specs, out_specs, scratch, operands, flops=0):
    return pl.pallas_call(
        kernel,
        out_shape=out_shape,
        in_specs=in_specs,
        out_specs=out_specs,
        scratch_shapes=scratch,
        cost_estimate=pl.CostEstimate(flops=flops, bytes_accessed=1 << 20, transcendentals=0),
        compiler_params=pltpu.CompilerParams(vmem_limit_bytes=VMEM_LIMIT),
    )(*operands)


def main(core, first, other):
    half = bf16(CHIPS, PAIR, HEAD_SIZE)
    return call(
        main_kernel, (half, half, half),
        [SMEM, VMEM, VMEM], (VMEM, VMEM, VMEM),
        [pltpu.SMEM((CHIPS,), jnp.int32)] * 2
        + [pltpu.VMEM((CHIPS, PAIR), jnp.int32)]
        + [pltpu.VMEM((REACH + CHIPS + 1, ROWS, HEAD_SIZE), jnp.float32)] * 4
        + [pltpu.VMEM((WIDEST * ROWS, PAIR), jnp.float32)] * (3 * AT_ONCE),
        (core, first, other),
        flops=1 << 32,
    )


def body(queries, keys, values, dout, segments):
    swap = [(i, i ^ 1) for i in range(CHIPS * CORES)]
    planes = [[CORES * n + c for n in range(CHIPS)] for c in range(CORES)]
    core = (lax.axis_index("blk") % CORES).astype(jnp.int32).reshape(1)
    packed = call(
        pack_kernel, bf16(CHIPS, IN_ROWS, HEAD_SIZE), [HBM] * 5, VMEM,
        [
            pltpu.VMEM((ROWS, 2 * CHIPS * HEAD_SIZE), jnp.bfloat16),
            pltpu.VMEM((ROWS, CHIPS * HEAD_SIZE), jnp.bfloat16),
            pltpu.VMEM((ROWS, CHIPS * HEAD_SIZE), jnp.bfloat16),
            pltpu.VMEM((ROWS, 2 * CHIPS * HEAD_SIZE), jnp.bfloat16),
            pltpu.VMEM((1, ROWS), jnp.int32),
            pltpu.SemaphoreType.DMA((5,)),
        ],
        [
            pltpu.with_memory_space_constraint(a, pltpu.HBM)
            for a in (queries, keys, values, dout, segments.reshape(1, ROWS))
        ],
    )
    first = lax.all_to_all(packed, "blk", 0, 0, tiled=True, axis_index_groups=planes)
    other = lax.ppermute(first[:, KV_AT:, :], "blk", swap)
    dq, keep, send = main(core, first, other)
    got = lax.ppermute(send, "blk", swap)
    joined = call(
        join_kernel, bf16(CHIPS, 2 * PAIR, HEAD_SIZE), [VMEM] * 3, VMEM, [], (dq, keep, got)
    )
    back = lax.all_to_all(joined, "blk", 0, 0, tiled=True, axis_index_groups=planes)
    narrow = bf16(ROWS, CHIPS * HEAD_SIZE)
    return call(
        unpack_kernel, (bf16(ROWS, 2 * CHIPS * HEAD_SIZE), narrow, narrow), [VMEM], (HBM,) * 3,
        [
            pltpu.VMEM((ROWS, 2 * CHIPS * HEAD_SIZE), jnp.bfloat16),
            pltpu.VMEM((ROWS, CHIPS * HEAD_SIZE), jnp.bfloat16),
            pltpu.VMEM((ROWS, CHIPS * HEAD_SIZE), jnp.bfloat16),
            pltpu.SemaphoreType.DMA((3,)),
        ],
        (back,),
    )


def solution(mesh):
    rows = P(("grp", "blk"), None)
    in_specs = (rows, rows, rows, rows, P(("grp", "blk")))
    return jax.shard_map(body, mesh=mesh, in_specs=in_specs, out_specs=(rows, rows, rows), check_vma=False)
```

time: 61.7 us -> 60.6 us (0.982)
  no operation moved by 1% of the time
where the time goes in v4:
time: 60.6 us; the launch traced here: 60.4 us
  blocking collectives  44.3 us (73%)
  Pallas kernels  9 us (15%)
  starting transfers between devices  3.22 us (5%)
  waiting for transfers between devices  3.12 us (5%)
  between operations  0.66 us (1%)
    all_to_all x1, blocking collectives, body(): lax.all_to_all(packed, 'blk', 0, 0, tiled=True, axis_index_groups=planes)  26.5 us
    all_to_all x1, blocking collectives, body(): lax.all_to_all(joined, 'blk', 0, 0, tiled=True, axis_index_groups=planes)  17.8 us
    pallas_call x4, Pallas kernels, call(): pl.pallas_call(kernel, out_shape=out_shape, in_specs=in_specs, out_specs=...  9 us
    ppermute x1, starting transfers between devices, body(): other = lax.ppermute(first[:, KV_AT:, :], 'blk', swap)  2.2 us
    ppermute x1, waiting for transfers between devices, body(): other = lax.ppermute(first[:, KV_AT:, :], 'blk', swap)  1.58 us
    ppermute x1, waiting for transfers between devices, body(): got = lax.ppermute(send, 'blk', swap)  1.54 us
  transfers between devices with their start and end apart: 2, of which 2 were waited for; matrix products, arithmetic and copies ran while one was open for 0% of the time, Pallas kernels for 0%

profile of v4, /device:TPU:1, one launch (start us, length us, event | category | flops | bytes accessed | tf_op | source)
XLA Modules:
  0.0 60.4 jit_solution(18149994059492525563)
XLA Ops:
  0.6 1.4 %shard_map.76 = bf16[8,784,128]{2,1,0:T(8,128)(2,1)S(1)} custom-call(bf16[128,2048]{1,0:T(8,128)(2,1)} %q_ref.1, bf16[128,1024]{1,0:T(8,128)(2,1)} %k_ref.1, bf16[128,1024]{1,0:T(8,128)(2,1)} %v_ref.1, bf16[128,2048]{1,0:T(8,128)(2,1)} %do_ref.1, s32[1,128]{1,0:T(1,128)} %bitcast.2), custom_call_target="tpu_custom_call" | custom-call | bytes 1048576 | tf_op jit(solution)/shard_map/pallas_call | solution.py:213
  2.1 26.5 %all_to_all.10.in_ref = bf16[8,784,128]{2,1,0:T(8,128)(2,1)S(1)} all-to-all(bf16[8,784,128]{2,1,0:T(8,128)(2,1)S(1)} %shard_map.76), channel_id=1, replica_groups={{0,2,4,6,8,10,12,14},{1,3,5,7,9,11,13,15},{16,18,20,22,24,26,28,30},{17..., dimensions={0} | all-to-all | bytes 3211264 | tf_op jit(solution)/shard_map/all_to_all | solution.py:257
  28.6 2.2 %collective-permute-start = (bf16[8,272,128]{2,1,0:T(8,128)(2,1)S(1)}, bf16[8,272,128]{2,1,0:T(8,128)(2,1)S(1)}, u32[]{:S(2)}, u32[]{:S(2)}) collective-permute-start(bf16[8,272,128]{2,1,0:T(8,128)(2,1)S(1)} %slice.4), channel_id=1, source_target_pairs={{0,1},{1,0},{2,3},{3,2},{4,5},{5,4},{6,7},{7,6},{8,9},{9,8},{10,11... | collective-permute-start | bytes 1671176 | tf_op jit(solution)/shard_map/ppermute | solution.py:258
  30.8 1.6 %collective-permute-done.other_ref = bf16[8,272,128]{2,1,0:T(8,128)(2,1)S(1)} collective-permute-done((bf16[8,272,128]{2,1,0:T(8,128)(2,1)S(1)}, bf16[8,272,128]{2,1,0:T(8,128)(2,1)S(1)}, u32[]{:S(2)}, u32[]{:S(2)}) %collective-permute-start) | collective-permute-done | bytes 557088 | tf_op jit(solution)/shard_map/ppermute | solution.py:258
  32.4 6.3 %shard_map.77 = (bf16[8,256,128]{2,1,0:T(8,128)(2,1)S(1)}, bf16[8,256,128]{2,1,0:T(8,128)(2,1)S(1)}, bf16[8,256,128]{2,1,0:T(8,128)(2,1)S(1)}) custom-call(s32[1]{0:T(128)} %bitcast.core_ref, bf16[8,784,128]{2,1,0:T(8,128)(2,1)S(1)} %all_to_all.10.in_ref, bf16[8,272,128]{2,1,0:T(8,128)(2,1)S(1)} %collective-permute-done.other_ref), custom_call_target="tpu_custom_call" | custom-call | flops 4294967296 | bytes 1048576 | tf_op jit(solution)/shard_map/pallas_call | solution.py:213
  38.7 1.0 %collective-permute-start.1 = (bf16[8,256,128]{2,1,0:T(8,128)(2,1)S(1)}, bf16[8,256,128]{2,1,0:T(8,128)(2,1)S(1)}, u32[]{:S(2)}, u32[]{:S(2)}) collective-permute-start(bf16[8,256,128]{2,1,0:T(8,128)(2,1)S(1)} %get-tuple-element.8), channel_id=1, source_target_pairs={{0,1},{1,0},{2,3},{3,2},{4,5},{5,4},{6,7},{7,6},{8,9},{9,8},{10,11... | collective-permute-start | bytes 1572872 | tf_op jit(solution)/shard_map/ppermute | solution.py:260
  39.7 1.5 %collective-permute-done.1.got_ref = bf16[8,256,128]{2,1,0:T(8,128)(2,1)S(1)} collective-permute-done((bf16[8,256,128]{2,1,0:T(8,128)(2,1)S(1)}, bf16[8,256,128]{2,1,0:T(8,128)(2,1)S(1)}, u32[]{:S(2)}, u32[]{:S(2)}) %collective-permute-start.1) | collective-permute-done | bytes 524320 | tf_op jit(solution)/shard_map/ppermute | solution.py:260
  41.3 0.2 shard_map.78
  41.4 17.8 %all_to_all.11.in_ref = bf16[8,512,128]{2,1,0:T(8,128)(2,1)S(1)} all-to-all(bf16[8,512,128]{2,1,0:T(8,128)(2,1)S(1)} %shard_map.78), channel_id=1, replica_groups={{0,2,4,6,8,10,12,14},{1,3,5,7,9,11,13,15},{16,18,20,22,24,26,28,30},{17..., dimensions={0} | all-to-all | bytes 2097152 | tf_op jit(solution)/shard_map/all_to_all | solution.py:264
  59.2 1.1 %shard_map.79 = (bf16[128,2048]{1,0:T(8,128)(2,1)}, bf16[128,1024]{1,0:T(8,128)(2,1)}, bf16[128,1024]{1,0:T(8,128)(2,1)}) custom-call(bf16[8,512,128]{2,1,0:T(8,128)(2,1)S(1)} %all_to_all.11.in_ref), custom_call_target="tpu_custom_call" | custom-call | bytes 1048576 | tf_op jit(solution)/shard_map/pallas_call | solution.py:213
  (1 shorter events, 0.0 us)
Async XLA Ops:
  28.6 3.8 %collective-permute-start = (bf16[8,272,128]{2,1,0:T(8,128)(2,1)S(1)}, bf16[8,272,128]{2,1,0:T(8,128)(2,1)S(1)}, u32[]{:S(2)}, u32[]{:S(2)}) collective-permute-start(bf16[8,272,128]{2,1,0:T(8,128)(2,1)S(1)} %slice.4), channel_id=1, source_target_pairs={{0,1},{1,0},{2,3},{3,2},{4,5},{5,4},{6,7},{7,6},{8,9},{9,8},{10,11... | collective-permute-start | bytes 1671176 | tf_op jit(solution)/shard_map/ppermute | solution.py:258
  38.7 2.6 %collective-permute-start.1 = (bf16[8,256,128]{2,1,0:T(8,128)(2,1)S(1)}, bf16[8,256,128]{2,1,0:T(8,128)(2,1)S(1)}, u32[]{:S(2)}, u32[]{:S(2)}) collective-permute-start(bf16[8,256,128]{2,1,0:T(8,128)(2,1)S(1)} %get-tuple-element.8), channel_id=1, source_target_pairs={{0,1},{1,0},{2,3},{3,2},{4,5},{5,4},{6,7},{7,6},{8,9},{9,8},{10,11... | collective-permute-start | bytes 1572872 | tf_op jit(solution)/shard_map/ppermute | solution.py:260

commit v5 on v4

--- a/solution.py
+++ b/solution.py
@@ -21,6 +21,7 @@
 TOKENS = CHIPS * PAIR
 WIDEST = 9
 REACH = 4
+LESS = 2
 AT_ONCE = 2
 
 score_scale = 1.0 / 12.0
@@ -143,12 +144,13 @@
         order_ref[rank] = n
         width_ref[rank] = widths[n]
 
-    def tiles_at_once(first_at, width):
+    def tiles_at_once(first_at, less, width):
+        widths = (width - less, width)
         tiles = [order_ref[first_at + u] for u in range(AT_ONCE)]
         q = [in_ref[n, 0:PAIR, :] for n in tiles]
         do = [in_ref[n, DO_AT : DO_AT + PAIR, :] for n in tiles]
         start = [first_s[pl.ds(n, 1), :] for n in tiles]
-        seen = [list(seen_blocks(n, core, width, in_ref, other_ref)) for n in tiles]
+        seen = [list(seen_blocks(n, core, w, in_ref, other_ref)) for n, w in zip(tiles, widths)]
         key_at = lax.broadcasted_iota(jnp.int32, (ROWS, PAIR), 0)
         query_at = lax.broadcasted_iota(jnp.int32, (ROWS, PAIR), 1) % ROWS
         total = [jnp.zeros((8, PAIR), jnp.float32) for _ in tiles]
@@ -156,6 +158,8 @@
         for j in range(width):
             at = pl.ds(j * ROWS, ROWS)
             for u in range(AT_ONCE):
+                if j >= widths[u]:
+                    continue
                 e_s, g_s, dp_s = work[3 * u : 3 * u + 3]
                 _, block, _, k, v = seen[u][j]
                 raw = lax.dot_general(k[...], q[u], NT, preferred_element_type=jnp.float32)
@@ -176,7 +180,7 @@
         delta = [jnp.sum(x, axis=0, keepdims=True) * y for x, y in zip(delta, inverse)]
         for u in range(AT_ONCE):
             e_s, g_s, dp_s = work[3 * u : 3 * u + 3]
-            for j in range(width):
+            for j in range(widths[u]):
                 at = pl.ds(j * ROWS, ROWS)
                 prob = e_s[at, :] * inverse[u]
                 low = prob.astype(jnp.bfloat16)
@@ -196,7 +200,23 @@
     @pl.loop(0, CHIPS // AT_ONCE)
     def _(group):
         first_at = group * AT_ONCE
-        by_width(width_ref[first_at + AT_ONCE - 1], functools.partial(tiles_at_once, first_at))
+        widest = width_ref[first_at + 1]
+        gap = widest - width_ref[first_at]
+
+        def pair(width):
+            if width <= LESS:
+                tiles_at_once(first_at, 0, width)
+                return
+
+            @pl.when(gap < LESS)
+            def _():
+                tiles_at_once(first_at, 0, width)
+
+            @pl.when(gap >= LESS)
+            def _():
+                tiles_at_once(first_at, LESS, width)
+
+        by_width(widest, pair)
 
     for ref, dk, dv in zip((keep_ref, send_ref), dk_s, dv_s):
         ref[:, 0:ROWS, :] = (dk[REACH : REACH + CHIPS] * score_scale).astype(jnp.bfloat16)

time: 60.6 us -> 60.1 us (level)
  Pallas kernels: 9 us -> 8.23 us
    pallas_call x4, Pallas kernels: 9 us -> 8.23 us  [call(): pl.pallas_call(kernel, out_shape=out_shape, in_specs=in_specs, out_specs=...]
where the time goes in v5:
time: 60.1 us; the launch traced here: 59.8 us
  blocking collectives  44.3 us (74%)
  Pallas kernels  8.23 us (14%)
  starting transfers between devices  3.43 us (6%)
  waiting for transfers between devices  3.12 us (5%)
  between operations  0.66 us (1%)
    all_to_all x1, blocking collectives, body(): lax.all_to_all(packed, 'blk', 0, 0, tiled=True, axis_index_groups=planes)  26.5 us
    all_to_all x1, blocking collectives, body(): lax.all_to_all(joined, 'blk', 0, 0, tiled=True, axis_index_groups=planes)  17.8 us
    pallas_call x4, Pallas kernels, call(): pl.pallas_call(kernel, out_shape=out_shape, in_specs=in_specs, out_specs=...  8.23 us
    ppermute x1, starting transfers between devices, body(): other = lax.ppermute(first[:, KV_AT:, :], 'blk', swap)  2.2 us
    ppermute x1, waiting for transfers between devices, body(): other = lax.ppermute(first[:, KV_AT:, :], 'blk', swap)  1.58 us
    ppermute x1, waiting for transfers between devices, body(): got = lax.ppermute(send, 'blk', swap)  1.54 us
    ppermute x1, starting transfers between devices, body(): got = lax.ppermute(send, 'blk', swap)  1.23 us
  transfers between devices with their start and end apart: 2, of which 2 were waited for; matrix products, arithmetic and copies ran while one was open for 0% of the time, Pallas kernels for 0%

profile of v5, /device:TPU:1, one launch (start us, length us, event | category | flops | bytes accessed | tf_op | source)
XLA Modules:
  0.0 59.8 jit_solution(17286619656756509467)
XLA Ops:
  0.6 1.4 %shard_map.76 = bf16[8,784,128]{2,1,0:T(8,128)(2,1)S(1)} custom-call(bf16[128,2048]{1,0:T(8,128)(2,1)} %q_ref.1, bf16[128,1024]{1,0:T(8,128)(2,1)} %k_ref.1, bf16[128,1024]{1,0:T(8,128)(2,1)} %v_ref.1, bf16[128,2048]{1,0:T(8,128)(2,1)} %do_ref.1, s32[1,128]{1,0:T(1,128)} %bitcast.2), custom_call_target="tpu_custom_call" | custom-call | bytes 1048576 | tf_op jit(solution)/shard_map/pallas_call | solution.py:233
  2.1 26.5 %all_to_all.10.in_ref = bf16[8,784,128]{2,1,0:T(8,128)(2,1)S(1)} all-to-all(bf16[8,784,128]{2,1,0:T(8,128)(2,1)S(1)} %shard_map.76), channel_id=1, replica_groups={{0,2,4,6,8,10,12,14},{1,3,5,7,9,11,13,15},{16,18,20,22,24,26,28,30},{17..., dimensions={0} | all-to-all | bytes 3211264 | tf_op jit(solution)/shard_map/all_to_all | solution.py:277
  28.6 2.2 %collective-permute-start = (bf16[8,272,128]{2,1,0:T(8,128)(2,1)S(1)}, bf16[8,272,128]{2,1,0:T(8,128)(2,1)S(1)}, u32[]{:S(2)}, u32[]{:S(2)}) collective-permute-start(bf16[8,272,128]{2,1,0:T(8,128)(2,1)S(1)} %slice.4), channel_id=1, source_target_pairs={{0,1},{1,0},{2,3},{3,2},{4,5},{5,4},{6,7},{7,6},{8,9},{9,8},{10,11... | collective-permute-start | bytes 1671176 | tf_op jit(solution)/shard_map/ppermute | solution.py:278
  30.8 1.6 %collective-permute-done.other_ref = bf16[8,272,128]{2,1,0:T(8,128)(2,1)S(1)} collective-permute-done((bf16[8,272,128]{2,1,0:T(8,128)(2,1)S(1)}, bf16[8,272,128]{2,1,0:T(8,128)(2,1)S(1)}, u32[]{:S(2)}, u32[]{:S(2)}) %collective-permute-start) | collective-permute-done | bytes 557088 | tf_op jit(solution)/shard_map/ppermute | solution.py:278
  32.4 5.5 %shard_map.77 = (bf16[8,256,128]{2,1,0:T(8,128)(2,1)S(1)}, bf16[8,256,128]{2,1,0:T(8,128)(2,1)S(1)}, bf16[8,256,128]{2,1,0:T(8,128)(2,1)S(1)}) custom-call(s32[1]{0:T(128)} %bitcast.core_ref, bf16[8,784,128]{2,1,0:T(8,128)(2,1)S(1)} %all_to_all.10.in_ref, bf16[8,272,128]{2,1,0:T(8,128)(2,1)S(1)} %collective-permute-done.other_ref), custom_call_target="tpu_custom_call" | custom-call | flops 4294967296 | bytes 1048576 | tf_op jit(solution)/shard_map/pallas_call | solution.py:233
  37.9 1.2 %collective-permute-start.1 = (bf16[8,256,128]{2,1,0:T(8,128)(2,1)S(1)}, bf16[8,256,128]{2,1,0:T(8,128)(2,1)S(1)}, u32[]{:S(2)}, u32[]{:S(2)}) collective-permute-start(bf16[8,256,128]{2,1,0:T(8,128)(2,1)S(1)} %get-tuple-element.8), channel_id=1, source_target_pairs={{0,1},{1,0},{2,3},{3,2},{4,5},{5,4},{6,7},{7,6},{8,9},{9,8},{10,11... | collective-permute-start | bytes 1572872 | tf_op jit(solution)/shard_map/ppermute | solution.py:280
  39.2 1.5 %collective-permute-done.1.got_ref = bf16[8,256,128]{2,1,0:T(8,128)(2,1)S(1)} collective-permute-done((bf16[8,256,128]{2,1,0:T(8,128)(2,1)S(1)}, bf16[8,256,128]{2,1,0:T(8,128)(2,1)S(1)}, u32[]{:S(2)}, u32[]{:S(2)}) %collective-permute-start.1) | collective-permute-done | bytes 524320 | tf_op jit(solution)/shard_map/ppermute | solution.py:280
  40.7 0.2 shard_map.78
  40.8 17.8 %all_to_all.11.in_ref = bf16[8,512,128]{2,1,0:T(8,128)(2,1)S(1)} all-to-all(bf16[8,512,128]{2,1,0:T(8,128)(2,1)S(1)} %shard_map.78), channel_id=1, replica_groups={{0,2,4,6,8,10,12,14},{1,3,5,7,9,11,13,15},{16,18,20,22,24,26,28,30},{17..., dimensions={0} | all-to-all | bytes 2097152 | tf_op jit(solution)/shard_map/all_to_all | solution.py:284
  58.7 1.1 %shard_map.79 = (bf16[128,2048]{1,0:T(8,128)(2,1)}, bf16[128,1024]{1,0:T(8,128)(2,1)}, bf16[128,1024]{1,0:T(8,128)(2,1)}) custom-call(bf16[8,512,128]{2,1,0:T(8,128)(2,1)S(1)} %all_to_all.11.in_ref), custom_call_target="tpu_custom_call" | custom-call | bytes 1048576 | tf_op jit(solution)/shard_map/pallas_call | solution.py:233
  (1 shorter events, 0.0 us)
Async XLA Ops:
  28.6 3.8 %collective-permute-start = (bf16[8,272,128]{2,1,0:T(8,128)(2,1)S(1)}, bf16[8,272,128]{2,1,0:T(8,128)(2,1)S(1)}, u32[]{:S(2)}, u32[]{:S(2)}) collective-permute-start(bf16[8,272,128]{2,1,0:T(8,128)(2,1)S(1)} %slice.4), channel_id=1, source_target_pairs={{0,1},{1,0},{2,3},{3,2},{4,5},{5,4},{6,7},{7,6},{8,9},{9,8},{10,11... | collective-permute-start | bytes 1671176 | tf_op jit(solution)/shard_map/ppermute | solution.py:278
  37.9 2.8 %collective-permute-start.1 = (bf16[8,256,128]{2,1,0:T(8,128)(2,1)S(1)}, bf16[8,256,128]{2,1,0:T(8,128)(2,1)S(1)}, u32[]{:S(2)}, u32[]{:S(2)}) collective-permute-start(bf16[8,256,128]{2,1,0:T(8,128)(2,1)S(1)} %get-tuple-element.8), channel_id=1, source_target_pairs={{0,1},{1,0},{2,3},{3,2},{4,5},{5,4},{6,7},{7,6},{8,9},{9,8},{10,11... | collective-permute-start | bytes 1572872 | tf_op jit(solution)/shard_map/ppermute | solution.py:280

commit v6 on v5

--- a/solution.py
+++ b/solution.py
@@ -80,7 +80,9 @@
     for m in range(CHIPS):
         for part in range(2):
             dq_s[:, columns(2 * m + part)] = in_ref[m, part * ROWS : (part + 1) * ROWS, :]
-    send(dq_s, dq_ref)
+        if m % 4 == 3:
+            wide = pl.ds((m - 3) * PAIR, 4 * PAIR)
+            send(dq_s.at[:, wide], dq_ref.at[:, wide])
     for held, out, at in ((dk_s, dk_ref, PAIR), (dv_s, dv_ref, PAIR + ROWS)):
         for m in range(CHIPS):
             held[:, columns(m)] = in_ref[m, at : at + ROWS, :]
@@ -289,7 +291,7 @@
             pltpu.VMEM((ROWS, 2 * CHIPS * HEAD_SIZE), jnp.bfloat16),
             pltpu.VMEM((ROWS, CHIPS * HEAD_SIZE), jnp.bfloat16),
             pltpu.VMEM((ROWS, CHIPS * HEAD_SIZE), jnp.bfloat16),
-            pltpu.SemaphoreType.DMA((3,)),
+            pltpu.SemaphoreType.DMA((4,)),
         ],
         (back,),
     )

time: 60.1 us -> 60.3 us (level)
  starting transfers between devices: 3.43 us -> 2.3 us
  Pallas kernels: 8.23 us -> 8.93 us
    ppermute x1, starting transfers between devices: 1.23 us -> 0.09 us  [body(): got = lax.ppermute(send, 'blk', swap)]
    pallas_call x4, Pallas kernels: 8.23 us -> 8.93 us  [call(): pl.pallas_call(kernel, out_shape=out_shape, in_specs=in_specs, out_specs=...]
where the time goes in v6:
time: 60.3 us; the launch traced here: 60 us
  blocking collectives  44.6 us (74%)
  Pallas kernels  8.93 us (15%)
  waiting for transfers between devices  3.48 us (6%)
  starting transfers between devices  2.3 us (4%)
  between operations  0.67 us (1%)
    all_to_all x1, blocking collectives, body(): lax.all_to_all(packed, 'blk', 0, 0, tiled=True, axis_index_groups=planes)  26.5 us
    all_to_all x1, blocking collectives, body(): lax.all_to_all(joined, 'blk', 0, 0, tiled=True, axis_index_groups=planes)  18.1 us
    pallas_call x4, Pallas kernels, call(): pl.pallas_call(kernel, out_shape=out_shape, in_specs=in_specs, out_specs=...  8.93 us
    ppermute x1, starting transfers between devices, body(): other = lax.ppermute(first[:, KV_AT:, :], 'blk', swap)  2.2 us
    ppermute x1, waiting for transfers between devices, body(): got = lax.ppermute(send, 'blk', swap)  1.9 us
    ppermute x1, waiting for transfers between devices, body(): other = lax.ppermute(first[:, KV_AT:, :], 'blk', swap)  1.58 us
  transfers between devices with their start and end apart: 2, of which 2 were waited for; matrix products, arithmetic and copies ran while one was open for 0% of the time, Pallas kernels for 0%

profile of v6, /device:TPU:1, one launch (start us, length us, event | category | flops | bytes accessed | tf_op | source)
XLA Modules:
  0.0 60.0 jit_solution(11706993591674134833)
XLA Ops:
  0.6 1.4 %shard_map.76 = bf16[8,784,128]{2,1,0:T(8,128)(2,1)S(1)} custom-call(bf16[128,2048]{1,0:T(8,128)(2,1)} %q_ref.1, bf16[128,1024]{1,0:T(8,128)(2,1)} %k_ref.1, bf16[128,1024]{1,0:T(8,128)(2,1)} %v_ref.1, bf16[128,2048]{1,0:T(8,128)(2,1)} %do_ref.1, s32[1,128]{1,0:T(1,128)} %bitcast.2), custom_call_target="tpu_custom_call" | custom-call | bytes 1048576 | tf_op jit(solution)/shard_map/pallas_call | solution.py:235
  2.1 26.5 %all_to_all.10.in_ref = bf16[8,784,128]{2,1,0:T(8,128)(2,1)S(1)} all-to-all(bf16[8,784,128]{2,1,0:T(8,128)(2,1)S(1)} %shard_map.76), channel_id=1, replica_groups={{0,2,4,6,8,10,12,14},{1,3,5,7,9,11,13,15},{16,18,20,22,24,26,28,30},{17..., dimensions={0} | all-to-all | bytes 3211264 | tf_op jit(solution)/shard_map/all_to_all | solution.py:279
  28.6 2.2 %collective-permute-start = (bf16[8,272,128]{2,1,0:T(8,128)(2,1)S(1)}, bf16[8,272,128]{2,1,0:T(8,128)(2,1)S(1)}, u32[]{:S(2)}, u32[]{:S(2)}) collective-permute-start(bf16[8,272,128]{2,1,0:T(8,128)(2,1)S(1)} %slice.4), channel_id=1, source_target_pairs={{0,1},{1,0},{2,3},{3,2},{4,5},{5,4},{6,7},{7,6},{8,9},{9,8},{10,11... | collective-permute-start | bytes 1671176 | tf_op jit(solution)/shard_map/ppermute | solution.py:280
  30.8 1.6 %collective-permute-done.other_ref = bf16[8,272,128]{2,1,0:T(8,128)(2,1)S(1)} collective-permute-done((bf16[8,272,128]{2,1,0:T(8,128)(2,1)S(1)}, bf16[8,272,128]{2,1,0:T(8,128)(2,1)S(1)}, u32[]{:S(2)}, u32[]{:S(2)}) %collective-permute-start) | collective-permute-done | bytes 557088 | tf_op jit(solution)/shard_map/ppermute | solution.py:280
  32.4 6.3 %shard_map.77 = (bf16[8,256,128]{2,1,0:T(8,128)(2,1)S(1)}, bf16[8,256,128]{2,1,0:T(8,128)(2,1)S(1)}, bf16[8,256,128]{2,1,0:T(8,128)(2,1)S(1)}) custom-call(s32[1]{0:T(128)} %bitcast.core_ref, bf16[8,784,128]{2,1,0:T(8,128)(2,1)S(1)} %all_to_all.10.in_ref, bf16[8,272,128]{2,1,0:T(8,128)(2,1)S(1)} %collective-permute-done.other_ref), custom_call_target="tpu_custom_call" | custom-call | flops 4294967296 | bytes 1048576 | tf_op jit(solution)/shard_map/pallas_call | solution.py:235
  38.7 0.1 collective-permute-start.1
  38.8 1.9 %collective-permute-done.1.got_ref = bf16[8,256,128]{2,1,0:T(8,128)(2,1)S(1)} collective-permute-done((bf16[8,256,128]{2,1,0:T(8,128)(2,1)S(1)}, bf16[8,256,128]{2,1,0:T(8,128)(2,1)S(1)}, u32[]{:S(2)}, u32[]{:S(2)}) %collective-permute-start.1) | collective-permute-done | bytes 524320 | tf_op jit(solution)/shard_map/ppermute | solution.py:282
  40.7 0.2 shard_map.78
  40.8 18.1 %all_to_all.11.in_ref = bf16[8,512,128]{2,1,0:T(8,128)(2,1)S(1)} all-to-all(bf16[8,512,128]{2,1,0:T(8,128)(2,1)S(1)} %shard_map.78), channel_id=1, replica_groups={{0,2,4,6,8,10,12,14},{1,3,5,7,9,11,13,15},{16,18,20,22,24,26,28,30},{17..., dimensions={0} | all-to-all | bytes 2097152 | tf_op jit(solution)/shard_map/all_to_all | solution.py:286
  58.9 1.1 %shard_map.79 = (bf16[128,2048]{1,0:T(8,128)(2,1)}, bf16[128,1024]{1,0:T(8,128)(2,1)}, bf16[128,1024]{1,0:T(8,128)(2,1)}) custom-call(bf16[8,512,128]{2,1,0:T(8,128)(2,1)S(1)} %all_to_all.11.in_ref), custom_call_target="tpu_custom_call" | custom-call | bytes 1048576 | tf_op jit(solution)/shard_map/pallas_call | solution.py:235
  (1 shorter events, 0.0 us)
Async XLA Ops:
  28.6 3.8 %collective-permute-start = (bf16[8,272,128]{2,1,0:T(8,128)(2,1)S(1)}, bf16[8,272,128]{2,1,0:T(8,128)(2,1)S(1)}, u32[]{:S(2)}, u32[]{:S(2)}) collective-permute-start(bf16[8,272,128]{2,1,0:T(8,128)(2,1)S(1)} %slice.4), channel_id=1, source_target_pairs={{0,1},{1,0},{2,3},{3,2},{4,5},{5,4},{6,7},{7,6},{8,9},{9,8},{10,11... | collective-permute-start | bytes 1671176 | tf_op jit(solution)/shard_map/ppermute | solution.py:280
  38.7 2.0 %collective-permute-start.1 = (bf16[8,256,128]{2,1,0:T(8,128)(2,1)S(1)}, bf16[8,256,128]{2,1,0:T(8,128)(2,1)S(1)}, u32[]{:S(2)}, u32[]{:S(2)}) collective-permute-start(bf16[8,256,128]{2,1,0:T(8,128)(2,1)S(1)} %get-tuple-element.8), channel_id=1, source_target_pairs={{0,1},{1,0},{2,3},{3,2},{4,5},{5,4},{6,7},{7,6},{8,9},{9,8},{10,11... | collective-permute-start | bytes 1572872 | tf_op jit(solution)/shard_map/ppermute | solution.py:282
